TPU v7x, 256 devices: a whole 4x4x8 slice. The times are simulated.
256 devices in a mesh: sta: 64 (over y, z, core), grp: 4 (over x).
Axes of the slice: x: 4, y: 4, z: 8, core: 2. Of those that a mesh axis runs over, the one named last changes fastest.
Arguments:
- records: bfloat16 [4096, 4096], P('grp', 'sta'), may hold values from -150 to 150
- pair_list: int32 [2048, 128, 2], P(('sta', 'grp')), may hold values from 0 to 4095, as said below
- live_blocks: int32 [256], P(('sta', 'grp')), may hold values from 1 to 8, as said below
Outputs:
- correlations: float32 [2048, 128, 1024], P(('sta', 'grp'))
Inputs may be any that keep to these rules, and one draw needn't show every extreme that they name: `pair_list`: each pair names two different stations. Writing a station as n * 1024 + c * 16 + k with 0 <= k < 16 (network n, column c), every pair of block b has its first station in column b // 32 and its second station in the same column or at most 2 columns higher. `live_blocks`: some device has all 8 slots in use; the slots in use on a device come first.
All inputs are finite; a program needn't handle non-finite values.
Results may differ from a plain program's by a relative error of at most 0.0073.
Values may be sent and summed in bfloat16 or wider, within the bound.
No kernel may reach another device: no remote copies, remote signals or barrier semaphores. Data moves between devices by JAX's collectives and lax.ppermute only.
A program may use at most 64 MiB of HBM per device.

v0:
```python
import math

import jax
import jax.numpy as jnp
from jax import lax
from jax.sharding import PartitionSpec as P

WINDOW_COUNT = 4
WINDOW_POINTS = 1024
HALF = 16
BLOCK = 128
GROUP = 4
REACH = 2
NF = 512


def from_behind(value, axis, by):
    count = lax.axis_size(axis)
    pairs = [(i, i + by) for i in range(count) if 0 <= i + by < count]
    return lax.ppermute(value, axis, pairs)


def forward_table(trace_duration, bin_count):
    impulse_moments = jnp.arange(trace_duration, dtype=jnp.int32)[:, None]
    spectral_position = jnp.arange(1, bin_count + 1, dtype=jnp.int32)[None, :]
    spectral_rotations = (impulse_moments * spectral_position % trace_duration).astype(
        jnp.float32
    ) * (2.0 * math.pi / trace_duration)
    factor = 1.0 / math.sqrt(trace_duration)
    return (
        jnp.concatenate([jnp.cos(spectral_rotations), -jnp.sin(spectral_rotations)], axis=1)
        * factor
    ).astype(jnp.bfloat16)


def lag_table(trace_duration, bin_count, segment_count):
    spectral_position = jnp.arange(1, bin_count + 1, dtype=jnp.int32)[:, None]
    lag_index = jnp.arange(trace_duration, dtype=jnp.int32)[None, :] - trace_duration // 2
    spectral_rotations = (spectral_position * lag_index % trace_duration).astype(jnp.float32) * (
        2.0 * math.pi / trace_duration
    )
    factor = 1.0 / math.sqrt(bin_count * segment_count)
    return (
        jnp.concatenate([jnp.cos(spectral_rotations), -jnp.sin(spectral_rotations)], axis=0)
        * factor
    ).astype(jnp.bfloat16)


def smoother(bin_count, half_width, segment_count):
    positions = jnp.arange(bin_count, dtype=jnp.int32)
    inside = (jnp.abs(positions[:, None] - positions[None, :]) <= half_width).astype(jnp.float32)
    totals = jnp.sum(inside, axis=0)
    return inside / (totals * segment_count)[None, :]


def whiten(segments, forward, weights):
    stations, segment_count, trace_duration = segments.shape
    bin_count = weights.shape[0]
    spectra = jnp.dot(
        segments.reshape(stations * segment_count, trace_duration),
        forward,
        preferred_element_type=jnp.float32,
    )
    spectra = spectra.reshape(stations, segment_count, 2 * bin_count)
    energy = jnp.sum(spectra * spectra, axis=1)
    energy = energy[:, :bin_count] + energy[:, bin_count:]
    disturbance_amplitudes = jnp.dot(energy, weights, precision=lax.Precision.HIGHEST)
    scaling = lax.rsqrt(disturbance_amplitudes + 1e-06)
    scaling = jnp.concatenate([scaling, scaling], axis=1)
    return (spectra * scaling[:, None, :]).astype(jnp.bfloat16)


def cross_spectra(first_rows, second_rows):
    bin_count = first_rows.shape[2] // 2
    first_re = first_rows[:, :, :bin_count].astype(jnp.float32)
    first_im = first_rows[:, :, bin_count:].astype(jnp.float32)
    second_re = second_rows[:, :, :bin_count].astype(jnp.float32)
    second_im = second_rows[:, :, bin_count:].astype(jnp.float32)
    real_part = jnp.sum(first_re * second_re + first_im * second_im, axis=1)
    imag_part = jnp.sum(first_im * second_re - first_re * second_im, axis=1)
    return jnp.concatenate([real_part, imag_part], axis=1).astype(jnp.bfloat16)


def select_rows(indices, table):
    positions = jnp.arange(table.shape[0], dtype=jnp.int32)
    onehot = (indices[:, None] == positions[None, :]).astype(jnp.bfloat16)
    return jnp.dot(onehot, table, preferred_element_type=jnp.float32).astype(jnp.bfloat16)


def local(records, pair_list, live_blocks):
    columns = lax.axis_size("sta")
    networks = lax.axis_size("grp")
    per_device = records.shape[0] // columns
    samples = records.shape[1]
    forward = forward_table(WINDOW_POINTS, NF)
    weights = smoother(NF, HALF, WINDOW_COUNT)
    arranged = records.reshape(columns, per_device, samples)
    received = lax.all_to_all(arranged, "sta", split_axis=0, concat_axis=2, tiled=True)
    whitened = whiten(
        received.reshape(received.shape[1], WINDOW_COUNT, WINDOW_POINTS), forward, weights
    )
    tile_block = lax.all_gather(whitened, "grp", axis=0, tiled=True)
    pieces = [tile_block]
    for offset in range(1, REACH + 1):
        pieces.append(from_behind(tile_block, "sta", -offset))
    window = jnp.concatenate(pieces, axis=0)
    tile_size = networks * per_device
    quarter_size = columns * per_device
    my_column = lax.axis_index("sta")
    flat_window = window.reshape(window.shape[0], WINDOW_COUNT * 2 * NF)
    own_tile = flat_window[:tile_size]

    def locate(station):
        network = station // quarter_size
        column = station % quarter_size // per_device
        return (column - my_column) * tile_size + network * per_device + station % per_device

    local_pairs = jnp.stack([locate(pair_list[:, :, 0]), locate(pair_list[:, :, 1])], axis=-1)
    block_cap = pair_list.shape[0]
    groups = local_pairs.reshape(block_cap // GROUP, GROUP * BLOCK, 2)
    inverse = lag_table(WINDOW_POINTS, NF, WINDOW_COUNT)

    def transform_group(group_rows):
        first_rows = select_rows(group_rows[:, 0], own_tile).reshape(-1, WINDOW_COUNT, 2 * NF)
        second_rows = select_rows(group_rows[:, 1], flat_window).reshape(-1, WINDOW_COUNT, 2 * NF)
        mixed_spectra = cross_spectra(first_rows, second_rows)
        return jnp.dot(mixed_spectra, inverse, preferred_element_type=jnp.float32)

    stacked = lax.map(transform_group, groups).reshape(block_cap, BLOCK, -1)
    keep_mask = (jnp.arange(block_cap, dtype=jnp.int32) < live_blocks[0]).astype(jnp.float32)
    return stacked * keep_mask[:, None, None]


def solution(mesh):
    in_specs = (P("grp", "sta"), P(("sta", "grp"), None, None), P(("sta", "grp")))
    out_specs = P(("sta", "grp"), None, None)
    return jax.shard_map(local, mesh=mesh, in_specs=in_specs, out_specs=out_specs, check_vma=False)
```

profile of v0, /device:TPU:6, one launch (start us, length us, event | category | flops | bytes accessed | tf_op | source)
XLA Modules:
  0.0 147.1 jit_solution(4232811175343725011)
XLA Ops:
  1.9 12.1 %all-to-all-start = ((bf16[64,2,512]{2,1,0:T(2,128)(2,1)}), bf16[64,2,512]{2,1,0:T(2,128)(2,1)S(1)}, u32[]{:S(2)}, u32[]{:S(2)}) async-start(bf16[64,2,512]{2,1,0:T(2,128)(2,1)} %reshape.49), calls=%async_computation | async-start | bytes 262144 | tf_op jit(solution)/shard_map/all_to_all | solution.py:98
  14.1 9.2 %fusion.28 = (f32[1024,512]{1,0:T(8,128)S(1)}, f32[1024,512]{1,0:T(8,128)}) fusion(s32[512]{0:T(512)S(1)} %iota_add_fusion.1), kind=kLoop, calls=%fused_computation.53 | loop fusion | flops 7864320 | bytes 4196352 | tf_op jit(solution)/shard_map/cos | solution.py:31
  24.8 2.1 %fusion.23 = f32[64,1024]{1,0:T(8,128)S(1)} fusion(bf16[64,1024]{1,0:T(8,128)(2,1)S(1)} %reshape_reshape.3, f32[1024,512]{1,0:T(8,128)} %get-tuple-element.59, f32[1024,512]{1,0:T(8,128)S(1)} %get-tuple-element.58), kind=kOutput, calls=%fused_computation.48 | convolution fusion | flops 137363456 | bytes 4587520 | tf_op jit(solution)/shard_map/dot_general | solution.py:59
  27.9 13.4 %all_gather.3 = bf16[64,4,1024]{2,1,0:T(4,128)(2,1)S(1)} all-gather(bf16[16,4,1024]{2,1,0:T(4,128)(2,1)S(1)} %multiply_convert_fusion), channel_id=1, replica_groups=mesh['sta'=64,'grp'=4] {'grp'}, dimensions={0}, use_global_device_ids=true | all-gather | bytes 655360 | tf_op jit(solution)/shard_map/all_gather | solution.py:102
  41.3 1.3 collective-permute-start
  42.6 1.5 %collective-permute-start.1 = (bf16[64,4,1024]{2,1,0:T(4,128)(2,1)S(1)}, bf16[64,4,1024]{2,1,0:T(4,128)(2,1)S(1)}, u32[]{:S(2)}, u32[]{:S(2)}) collective-permute-start(bf16[64,4,1024]{2,1,0:T(4,128)(2,1)S(1)} %all_gather.3), channel_id=1, source_target_pairs={{8,0},{12,4},{16,8},{20,12},{24,16},{28,20},{32,24},{36,28},{40,32... | collective-permute-start | bytes 1572872 | tf_op jit(solution)/shard_map/ppermute | solution.py:20
  44.1 8.3 %fusion.27 = (f32[512,1024]{1,0:T(8,128)S(1)}, f32[512,1024]{1,0:T(8,128)S(1)}) fusion(s32[1024]{0:T(1024)S(1)} %iota_add_fusion, s32[512]{0:T(512)S(1)} %iota_add_fusion.1), kind=kLoop, calls=%fused_computation.51 | loop fusion | flops 7864320 | bytes 4200448 | tf_op jit(solution)/shard_map/cos | solution.py:44
  52.4 2.0 %fusion.11 = bf16[1024,1024]{1,0:T(8,128)(2,1)} fusion(f32[512,1024]{1,0:T(8,128)S(1)} %get-tuple-element.57, f32[512,1024]{1,0:T(8,128)S(1)} %get-tuple-element.56), kind=kLoop, calls=%fused_computation.23 | loop fusion | flops 3145728 | bytes 6291456 | tf_op jit(solution)/shard_map/convert_element_type | solution.py:46
  54.5 8.5 %collective-permute-done.1 = bf16[64,4,1024]{2,1,0:T(4,128)(2,1)S(1)} collective-permute-done((bf16[64,4,1024]{2,1,0:T(4,128)(2,1)S(1)}, bf16[64,4,1024]{2,1,0:T(4,128)(2,1)S(1)}, u32[]{:S(2)}, u32[]{:S(2)}) %collective-permute-start.1) | collective-permute-done | bytes 524320 | tf_op jit(solution)/shard_map/ppermute | solution.py:20
  63.0 1.1 pad_maximum_fusion
  64.8 77.2 %while.10 = (s32[]{:T(128)}, f32[2,512,1024]{2,1,0:T(8,128)}, s32[2,512,2]{1,2,0:T(2,128)S(1)}, bf16[64,4096]{1,0:T(8,128)(2,1)S(1)}, bf16[192,4096]{1,0:T(8,128...) while((s32[]{:T(128)}, f32[2,512,1024]{2,1,0:T(8,128)}, s32[2,512,2]{1,2,0:T(2,128)S(1)}, ...), condition=%wide.region_5.6_spmd, body=%wide.region_2.5_spmd.sunk | while | flops 2165964800 | bytes 50352748 | solution.py:129
  64.8 3.3 %convolution_convert_fusion.4 = bf16[512,4096]{1,0:T(8,128)(2,1)} fusion(bf16[192,4096]{1,0:T(8,128)(2,1)S(1)} %get-tuple-element.123, s32[512]{0:T(512)S(1)} %bitcast.46), kind=kOutput, calls=%fused_computation.clone.1 | convolution fusion | flops 807501824 | bytes 5769216 | tf_op jit(solution)/shard_map/while/body/eval_jaxpr/dot_general | solution.py:87
  68.1 7.8 %reshape.53 = bf16[512,4,1024]{2,1,0:T(4,128)(2,1)} reshape(bf16[512,4096]{1,0:T(8,128)(2,1)} %convolution_convert_fusion.4) | data formatting | bytes 8388608 | tf_op jit(solution)/shard_map/while/body/eval_jaxpr/reshape | solution.py:125
  75.9 3.3 %convolution_convert_fusion.5 = bf16[512,4096]{1,0:T(8,128)(2,1)} fusion(bf16[64,4096]{1,0:T(8,128)(2,1)S(1)} %get-tuple-element.122, s32[512]{0:T(512)S(1)} %bitcast.45), kind=kOutput, calls=%fused_computation.1.clone.1 | convolution fusion | flops 270565376 | bytes 4720640 | tf_op jit(solution)/shard_map/while/body/eval_jaxpr/dot_general | solution.py:87
  79.2 7.8 %reshape.54 = bf16[512,4,1024]{2,1,0:T(4,128)(2,1)} reshape(bf16[512,4096]{1,0:T(8,128)(2,1)} %convolution_convert_fusion.5) | data formatting | bytes 8388608 | tf_op jit(solution)/shard_map/while/body/eval_jaxpr/reshape | solution.py:124
  87.0 13.8 %fusion.53 = (bf16[512,512]{1,0:T(8,128)(2,1)S(1)}, bf16[512,512]{1,0:T(8,128)(2,1)S(1)}) fusion(bf16[512,4,1024]{2,1,0:T(4,128)(2,1)} %reshape.53, bf16[512,4,1024]{2,1,0:T(4,128)(2,1)} %reshape.54), kind=kLoop, calls=%fused_computation.7.clone.1 | loop fusion | flops 12058624 | bytes 9437184 | tf_op jit(solution)/shard_map/while/body/eval_jaxpr/reduce_sum | solution.py:79
  100.8 2.6 %bitcast_dynamic-update-slice_fusion.2 = f32[2,512,1024]{2,1,0:T(8,128)} fusion(f32[2,512,1024]{2,1,0:T(8,128)} %get-tuple-element.113, s32[]{:T(128)} %get-tuple-element.112, bf16[1024,1024]{1,0:T(8,128)(2,1)S(1)} %copy-done, bf16[512,512]{1,0:T(8,128)(2,1)S(1)} %get-tuple-element.103, bf16[512,512]{1,0:T(8,128)(2,1)S(1)} %get-tuple-element.104), kind=kOutput, calls=%fused_computation.10.clone.1 | convolution fusion | flops 1075838976 | bytes 5243392 | tf_op jit(solution)/shard_map/while/body/eval_jaxpr/dot_general | solution.py:127
  103.4 3.3 %convolution_convert_fusion.4 = bf16[512,4096]{1,0:T(8,128)(2,1)} fusion(bf16[192,4096]{1,0:T(8,128)(2,1)S(1)} %get-tuple-element.123, s32[512]{0:T(512)S(1)} %bitcast.46), kind=kOutput, calls=%fused_computation.clone.1 | convolution fusion | flops 807501824 | bytes 5769216 | tf_op jit(solution)/shard_map/while/body/eval_jaxpr/dot_general | solution.py:87
  106.7 7.8 %reshape.53 = bf16[512,4,1024]{2,1,0:T(4,128)(2,1)} reshape(bf16[512,4096]{1,0:T(8,128)(2,1)} %convolution_convert_fusion.4) | data formatting | bytes 8388608 | tf_op jit(solution)/shard_map/while/body/eval_jaxpr/reshape | solution.py:125
  114.5 3.3 %convolution_convert_fusion.5 = bf16[512,4096]{1,0:T(8,128)(2,1)} fusion(bf16[64,4096]{1,0:T(8,128)(2,1)S(1)} %get-tuple-element.122, s32[512]{0:T(512)S(1)} %bitcast.45), kind=kOutput, calls=%fused_computation.1.clone.1 | convolution fusion | flops 270565376 | bytes 4720640 | tf_op jit(solution)/shard_map/while/body/eval_jaxpr/dot_general | solution.py:87
  117.8 7.8 %reshape.54 = bf16[512,4,1024]{2,1,0:T(4,128)(2,1)} reshape(bf16[512,4096]{1,0:T(8,128)(2,1)} %convolution_convert_fusion.5) | data formatting | bytes 8388608 | tf_op jit(solution)/shard_map/while/body/eval_jaxpr/reshape | solution.py:124
  125.6 13.8 %fusion.53 = (bf16[512,512]{1,0:T(8,128)(2,1)S(1)}, bf16[512,512]{1,0:T(8,128)(2,1)S(1)}) fusion(bf16[512,4,1024]{2,1,0:T(4,128)(2,1)} %reshape.53, bf16[512,4,1024]{2,1,0:T(4,128)(2,1)} %reshape.54), kind=kLoop, calls=%fused_computation.7.clone.1 | loop fusion | flops 12058624 | bytes 9437184 | tf_op jit(solution)/shard_map/while/body/eval_jaxpr/reduce_sum | solution.py:79
  139.4 2.6 %bitcast_dynamic-update-slice_fusion.2 = f32[2,512,1024]{2,1,0:T(8,128)} fusion(f32[2,512,1024]{2,1,0:T(8,128)} %get-tuple-element.113, s32[]{:T(128)} %get-tuple-element.112, bf16[1024,1024]{1,0:T(8,128)(2,1)S(1)} %copy-done, bf16[512,512]{1,0:T(8,128)(2,1)S(1)} %get-tuple-element.103, bf16[512,512]{1,0:T(8,128)(2,1)S(1)} %get-tuple-element.104), kind=kOutput, calls=%fused_computation.10.clone.1 | convolution fusion | flops 1075838976 | bytes 5243392 | tf_op jit(solution)/shard_map/while/body/eval_jaxpr/dot_general | solution.py:127
  142.0 5.1 %broadcast_multiply_fusion = f32[8,128,1024]{2,1,0:T(8,128)} fusion(f32[8,128,1024]{2,1,0:T(8,128)} %bitcast.10, f32[8]{0:T(128)S(1)} %compare_convert_fusion), kind=kLoop, calls=%fused_computation.38 | loop fusion | flops 1048576 | bytes 8388640 | tf_op jit(solution)/shard_map/mul | solution.py:131
  (32 shorter events, 4.5 us)
Async XLA Ops:
  1.9 22.4 %all-to-all-start = ((bf16[64,2,512]{2,1,0:T(2,128)(2,1)}), bf16[64,2,512]{2,1,0:T(2,128)(2,1)S(1)}, u32[]{:S(2)}, u32[]{:S(2)}) async-start(bf16[64,2,512]{2,1,0:T(2,128)(2,1)} %reshape.49), calls=%async_computation | async-start | bytes 262144 | tf_op jit(solution)/shard_map/all_to_all | solution.py:98
  14.1 9.2 %copy-start.1 = (s32[8,128,2]{1,2,0:T(2,128)S(1)}, s32[8,128,2]{1,2,0:T(2,128)}, u32[]{:S(2)}) copy-start(s32[8,128,2]{1,2,0:T(2,128)} %param.6) | copy-start | bytes 24580
  41.3 13.2 %collective-permute-start = (bf16[64,4,1024]{2,1,0:T(4,128)(2,1)S(1)}, bf16[64,4,1024]{2,1,0:T(4,128)(2,1)S(1)}, u32[]{:S(2)}, u32[]{:S(2)}) collective-permute-start(bf16[64,4,1024]{2,1,0:T(4,128)(2,1)S(1)} %all_gather.3), channel_id=1, source_target_pairs={{4,0},{8,4},{12,8},{16,12},{20,16},{24,20},{28,24},{32,28},{36,32}... | collective-permute-start | bytes 1572872 | tf_op jit(solution)/shard_map/ppermute | solution.py:20
  42.6 20.5 %collective-permute-start.1 = (bf16[64,4,1024]{2,1,0:T(4,128)(2,1)S(1)}, bf16[64,4,1024]{2,1,0:T(4,128)(2,1)S(1)}, u32[]{:S(2)}, u32[]{:S(2)}) collective-permute-start(bf16[64,4,1024]{2,1,0:T(4,128)(2,1)S(1)} %all_gather.3), channel_id=1, source_target_pairs={{8,0},{12,4},{16,8},{20,12},{24,16},{28,20},{32,24},{36,28},{40,32... | collective-permute-start | bytes 1572872 | tf_op jit(solution)/shard_map/ppermute | solution.py:20
  87.0 13.8 %copy-start = (bf16[1024,1024]{1,0:T(8,128)(2,1)S(1)}, bf16[1024,1024]{1,0:T(8,128)(2,1)}, u32[]{:S(2)}) copy-start(bf16[1024,1024]{1,0:T(8,128)(2,1)} %get-tuple-element.124) | copy-start | bytes 6291460 | tf_op jit(solution)/shard_map/while
  125.6 13.8 %copy-start = (bf16[1024,1024]{1,0:T(8,128)(2,1)S(1)}, bf16[1024,1024]{1,0:T(8,128)(2,1)}, u32[]{:S(2)}) copy-start(bf16[1024,1024]{1,0:T(8,128)(2,1)} %get-tuple-element.124) | copy-start | bytes 6291460 | tf_op jit(solution)/shard_map/while
where the time goes:
time: 148 us; the launch traced here: 147 us
  other arithmetic  53.8 us (36%)
  local copies, waits for them, and re-layouts  34.6 us (23%)
  matrix products  20.9 us (14%)
  starting transfers between devices  14.9 us (10%)
  blocking collectives  13.4 us (9%)
  waiting for transfers between devices  8.65 us (6%)
    reduce_sum x2, other arithmetic, cross_spectra(): real_part = jnp.sum(first_re * second_re + first_im * second_im, axis=1)  27.6 us
    reshape x2, local copies, waits for them, and re-layouts, transform_group(): select_rows(group_rows[:, 0], own_tile).reshape(-1, WINDOW_COUNT, 2 * NF)  15.7 us
    reshape x2, local copies, waits for them, and re-layouts, transform_group(): select_rows(group_rows[:, 1], flat_window).reshape(-1, WINDOW_COUNT, 2 * NF)  15.6 us
    all_gather x1, blocking collectives, local(): tile_block = lax.all_gather(whitened, 'grp', axis=0, tiled=True)  13.4 us
    dot_general x4, matrix products, select_rows(): jnp.dot(onehot, table, preferred_element_type=jnp.float32)  13 us
    all_to_all x1, starting transfers between devices, local(): lax.all_to_all(arranged, 'sta', split_axis=0, concat_axis=2, tiled=True)  12.1 us
    cos x1, other arithmetic, forward_table(): jnp.cos(spectral_rotations)  9.21 us
    ppermute x2, waiting for transfers between devices, from_behind(): return lax.ppermute(value, axis, pairs)  8.51 us
  transfers between devices with their start and end apart: 3, of which 2 were waited for; matrix products, arithmetic and copies ran while one was open for 14% of the time, Pallas kernels for 0%

commit v1 on v0

v1 whole, which is shorter than its diff:
```python
import math

import jax
import jax.numpy as jnp
import ml_dtypes
import numpy as np
from jax import lax
from jax.experimental import pallas as pl
from jax.experimental.pallas import tpu as pltpu
from jax.sharding import PartitionSpec as P

SEGMENTS = 4
POINTS = 1024
BINS = 512
HALF = 16
BLOCK = 128
NETS = 4
PER = 16
SLOTS = 3
ROWS = 32
LANES = 128
STEP_PAIRS = 256

BIN_ORDER = np.concatenate([np.arange(2, BINS + 1, 2), np.arange(1, BINS + 1, 2)])


def forward_table():
    t = np.arange(POINTS, dtype=np.int64)[:, None]
    turn = (t * BIN_ORDER[None, :] % POINTS) * (2.0 * math.pi / POINTS)
    table = np.concatenate([np.cos(turn), -np.sin(turn)], axis=1) / math.sqrt(POINTS)
    return table.astype(np.float32).astype(ml_dtypes.bfloat16)


def lag_tables():
    lag = np.arange(POINTS // 2, dtype=np.int64)[None, :] - POINTS // 2
    tables = []
    for bins in (BIN_ORDER[: BINS // 2], BIN_ORDER[BINS // 2 :]):
        turn = (bins[:, None] * lag % POINTS) * (2.0 * math.pi / POINTS)
        table = np.concatenate([np.cos(turn), -np.sin(turn)], axis=0) / math.sqrt(BINS * SEGMENTS)
        tables.append(table.astype(np.float32).astype(ml_dtypes.bfloat16))
    return tables


def band_tables():
    near = np.abs(BIN_ORDER[:, None] - BIN_ORDER[None, :]) <= HALF
    share = 1.0 / (near.sum(axis=0) * SEGMENTS)
    return near.astype(np.float32).astype(ml_dtypes.bfloat16), share.astype(np.float32)[None, :]


def pack_kernel(records_ref, out_ref):
    samples, stations = records_ref.shape
    own = records_ref[...].astype(jnp.float32)
    ahead = jnp.concatenate([own[:, 2 * PER :], own[:, : 2 * PER]], axis=1)
    both = jnp.concatenate([own, ahead], axis=0)
    for block in range(stations // LANES):
        part = both[:, block * LANES : (block + 1) * LANES]
        out_ref[block * LANES : (block + 1) * LANES, :] = part.T.astype(jnp.bfloat16)


def whiten_kernel(parts_ref, forward_ref, band_ref, share_ref, both_ref, given_ref, segs, wide):
    core = lax.rem(lax.axis_index("sta"), 2)
    low = lax.broadcasted_iota(jnp.int32, (PER, LANES), 1) < LANES // 2
    for e in range(SEGMENTS):
        for u in range(POINTS // LANES):
            row = (e * POINTS // LANES + u) * 2 * PER
            first = parts_ref[row : row + PER, :].astype(jnp.float32)
            second = parts_ref[row + PER : row + 2 * PER, :].astype(jnp.float32)
            near = jnp.where(low, first, pltpu.roll(second, LANES // 2, 1))
            far = jnp.where(low, pltpu.roll(first, LANES // 2, 1), second)
            segs[e * PER : (e + 1) * PER, u * LANES : (u + 1) * LANES] = near.astype(jnp.bfloat16)
            segs[(SEGMENTS + e) * PER : (SEGMENTS + e + 1) * PER, u * LANES : (u + 1) * LANES] = (
                far.astype(jnp.bfloat16)
            )
    spectra = jnp.dot(segs[...], forward_ref[...], preferred_element_type=jnp.float32)
    squares = (spectra * spectra).reshape(2, SEGMENTS, PER, 2 * BINS)
    energy = jnp.sum(squares, axis=1).reshape(2 * PER, 2 * BINS)
    energy = energy[:, :BINS] + energy[:, BINS:]
    top = energy.astype(jnp.bfloat16)
    rest = energy - top.astype(jnp.float32)
    middle = rest.astype(jnp.bfloat16)
    bottom = (rest - middle.astype(jnp.float32)).astype(jnp.bfloat16)
    split = jnp.concatenate([top, middle, bottom], axis=0)
    sums = jnp.dot(split, band_ref[...], preferred_element_type=jnp.float32)
    count = 2 * PER
    total = sums[:count] + (sums[count : 2 * count] + sums[2 * count :])
    scale = lax.rsqrt(total * share_ref[...] + 1e-06)
    for column in range(2):
        for e in range(SEGMENTS):
            for k in range(0, PER, 8):
                for part in range(2):
                    for j in range(BINS // LANES):
                        at = (column * SEGMENTS + e) * PER + k
                        lane = part * BINS + j * LANES
                        piece = (
                            spectra[at : at + 8, lane : lane + LANES]
                            * scale[column * PER + k : column * PER + k + 8, j * LANES : (j + 1) * LANES]
                        )
                        row = (column * PER + k) * ROWS + part * (ROWS // 2) + e * (BINS // LANES) + j
                        wide[pl.ds(row, 8, stride=ROWS), :] = piece
    size = PER * ROWS
    given = 1 - core
    given_rows = wide[pl.ds(pl.multiple_of(given * size, size), size), :].astype(jnp.bfloat16)
    other_rows = wide[pl.ds(pl.multiple_of(core * size, size), size), :].astype(jnp.bfloat16)
    both_ref[:size, :] = given_rows
    both_ref[size:, :] = other_rows
    given_ref[...] = given_rows


def pair_kernel(
    live_ref, index_ref, even_ref, odd_ref, p0, p1, p2, p3, s0, s1, s2, s3, out_ref, table, mixed
):
    step = pl.program_id(0)
    size = PER * ROWS
    half = ROWS // 4

    @pl.when(step == 0)
    def _():
        for net, (pieces, swapped) in enumerate(((p0, s0), (p1, s1), (p2, s2), (p3, s3))):
            for slot in range(SLOTS):
                source = swapped if slot == 2 else pieces
                start = 0 if slot == 2 else slot * size
                for k in range(PER):
                    table[(slot * NETS + net) * PER + k] = source[
                        start + k * ROWS : start + (k + 1) * ROWS, :
                    ].astype(jnp.float32)

    upper = lax.broadcasted_iota(jnp.int32, (8, LANES), 0) < 4

    def mix(q):
        packed = index_ref[step * STEP_PAIRS + q]
        i = packed & 255
        j = packed >> 8
        ar0, ar1 = table[i, 0:half], table[i, half : 2 * half]
        ai0, ai1 = table[i, 2 * half : 3 * half], table[i, 3 * half : 4 * half]
        br0, br1 = table[j, 0:half], table[j, half : 2 * half]
        bi0, bi1 = table[j, 2 * half : 3 * half], table[j, 3 * half : 4 * half]
        real = (ar0 * br0 + ar1 * br1) + (ai0 * bi0 + ai1 * bi1)
        imag = (ai0 * br0 + ai1 * br1) - (ar0 * bi0 + ar1 * bi1)
        turned = pltpu.roll(jnp.where(upper, imag, real), 4, 0)
        mixed[pl.ds(pl.multiple_of(q * 8, 8), 8), :] = jnp.where(upper, real, imag) + turned

    def some(g, carry):
        for q in range(8):
            mix(g * 8 + q)
        return carry

    lax.fori_loop(0, STEP_PAIRS // 8, some, 0)

    def rows_of(blocks):
        return jnp.concatenate(
            [mixed[pl.ds(b, STEP_PAIRS, stride=8), :].astype(jnp.bfloat16) for b in blocks], axis=1
        )

    even = jnp.dot(rows_of((0, 1, 4, 5)), even_ref[...], preferred_element_type=jnp.float32)
    odd = jnp.dot(rows_of((2, 3, 6, 7)), odd_ref[...], preferred_element_type=jnp.float32)
    for b in range(STEP_PAIRS // BLOCK):
        keep = (step * (STEP_PAIRS // BLOCK) + b < live_ref[0]).astype(jnp.float32)
        here = slice(b * BLOCK, (b + 1) * BLOCK)
        out_ref[here, : POINTS // 2] = (even[here] + odd[here]) * keep
        out_ref[here, POINTS // 2 :] = (even[here] - odd[here]) * keep


def local(records, pair_list, live_blocks):
    columns = lax.axis_size("sta")
    nets = lax.axis_size("grp")
    column = lax.axis_index("sta")
    net = lax.axis_index("grp")
    core = column % 2
    vmem = pl.BlockSpec(memory_space=pltpu.VMEM)
    smem = pl.BlockSpec(memory_space=pltpu.SMEM)
    messages = pl.pallas_call(
        pack_kernel,
        out_shape=jax.ShapeDtypeStruct((columns * PER, LANES), jnp.bfloat16),
        in_specs=[vmem],
        out_specs=vmem,
    )(records.T)
    received = lax.all_to_all(
        messages.reshape(columns, PER, LANES), "sta", split_axis=0, concat_axis=0, tiled=True
    ).reshape(columns * PER, LANES)
    band, share = band_tables()
    size = PER * ROWS
    both, given = pl.pallas_call(
        whiten_kernel,
        out_shape=(
            jax.ShapeDtypeStruct((2 * size, LANES), jnp.bfloat16),
            jax.ShapeDtypeStruct((size, LANES), jnp.bfloat16),
        ),
        in_specs=[vmem] * 4,
        out_specs=(vmem, vmem),
        scratch_shapes=[
            pltpu.VMEM((2 * SEGMENTS * PER, POINTS), jnp.bfloat16),
            pltpu.VMEM((2 * size, LANES), jnp.float32),
        ],
    )(received, jnp.asarray(forward_table()), jnp.asarray(band), jnp.asarray(share))
    swap = [(i, i ^ 1) for i in range(columns)]
    pieces, swapped = [both], [lax.ppermute(given, "sta", swap)]
    for by in range(1, nets):
        piece = lax.ppermute(both, "grp", [((i + by) % nets, i) for i in range(nets)])
        pieces.append(piece)
        swapped.append(lax.ppermute(piece[:size], "sta", swap))

    station_net = pair_list // (columns * PER)
    offset = pair_list // PER % columns - column
    slot = jnp.where(offset == 1, 2, jnp.where(offset == 0, 1 - core, core))
    place = (slot * nets + (station_net - net) % nets) * PER + pair_list % PER
    index = (place[:, :, 0] + 256 * place[:, :, 1]).reshape(-1)
    even, odd = lag_tables()
    pairs = index.shape[0]
    return pl.pallas_call(
        pair_kernel,
        grid=(pairs // STEP_PAIRS,),
        out_shape=jax.ShapeDtypeStruct((pairs, POINTS), jnp.float32),
        in_specs=[smem, smem] + [vmem] * 10,
        out_specs=pl.BlockSpec((STEP_PAIRS, POINTS), lambda i: (i, 0)),
        scratch_shapes=[
            pltpu.VMEM((SLOTS * NETS * PER, ROWS, LANES), jnp.float32),
            pltpu.VMEM((STEP_PAIRS * 8, LANES), jnp.float32),
        ],
        compiler_params=pltpu.CompilerParams(vmem_limit_bytes=40 * 2**20),
    )(live_blocks, index, jnp.asarray(even), jnp.asarray(odd), *pieces, *swapped).reshape(
        pair_list.shape[0], BLOCK, POINTS
    )


def solution(mesh):
    in_specs = (P("grp", "sta"), P(("sta", "grp"), None, None), P(("sta", "grp")))
    out_specs = P(("sta", "grp"), None, None)
    return jax.shard_map(local, mesh=mesh, in_specs=in_specs, out_specs=out_specs, check_vma=False)
```

time: 148 us -> 57.8 us (0.39)
  the two profiles are of different devices: /device:TPU:6 before, /device:TPU:1 now
where the time goes in v1:
time: 57.8 us; the launch traced here: 57.6 us
  blocking collectives  25.3 us (44%)
  Pallas kernels  13 us (22%)
  starting transfers between devices  9.06 us (16%)
  waiting for transfers between devices  7.74 us (13%)
  local copies, waits for them, and re-layouts  0.99 us (2%)
  other arithmetic  0.79 us (1%)
  between operations  0.69 us (1%)
    all_to_all x1, blocking collectives, local(): lax.all_to_all(messages.reshape(columns, PER, LANES), 'sta', split_axis=0...  25.3 us
    pallas_call x1, Pallas kernels, local(): pl.pallas_call(pair_kernel, grid=(pairs // STEP_PAIRS,), out_shape=jax.Sh...  7.59 us
    ppermute x3, waiting for transfers between devices, local(): lax.ppermute(both, 'grp', [((i + by) % nets, i) for i in range(nets)])  6.44 us
    ppermute x3, starting transfers between devices, local(): lax.ppermute(both, 'grp', [((i + by) % nets, i) for i in range(nets)])  4.82 us
    pallas_call x1, Pallas kernels, local(): pl.pallas_call(whiten_kernel, out_shape=(jax.ShapeDtypeStruct((2 * size,...  3.53 us
    ppermute x3, starting transfers between devices, local(): swapped.append(lax.ppermute(piece[:size], 'sta', swap))  2.86 us
    pallas_call x1, Pallas kernels, local(): pl.pallas_call(pack_kernel, out_shape=jax.ShapeDtypeStruct((columns * PER...  1.9 us
    ppermute x1, starting transfers between devices, local(): pieces, swapped = ([both], [lax.ppermute(given, 'sta', swap)])  1.38 us
  transfers between devices with their start and end apart: 7, of which 4 were waited for; matrix products, arithmetic and copies ran while one was open for 1% of the time, Pallas kernels for 0%

profile of v1, /device:TPU:1, one launch (start us, length us, event | category | flops | bytes accessed | tf_op | source)
XLA Modules:
  0.0 57.6 jit_solution(12746991409272848258)
XLA Ops:
  0.0 0.0 copy-start
  0.0 0.0 copy-start.1
  0.0 1.9 %shard_map.82 = bf16[1024,128]{1,0:T(8,128)(2,1)} custom-call(bf16[64,1024]{1,0:T(8,128)(2,1)} %bitcast.8), custom_call_target="tpu_custom_call" | custom-call | tf_op jit(solution)/shard_map/pallas_call | solution.py:171
  1.9 25.3 %all_to_all.5 = bf16[64,16,128]{2,1,0:T(8,128)(2,1)} all-to-all(bf16[64,16,128]{2,1,0:T(8,128)(2,1)} %bitcast.7), channel_id=1, replica_groups=mesh['sta'=64,'grp'=4] {'sta'}, dimensions={0} | all-to-all | bytes 524288 | tf_op jit(solution)/shard_map/all_to_all | solution.py:177
  27.2 3.5 %shard_map.83 = (bf16[1024,128]{1,0:T(8,128)(2,1)}, bf16[512,128]{1,0:T(8,128)(2,1)}) custom-call(bf16[1024,128]{1,0:T(8,128)(2,1)} %bitcast.6, bf16[1024,1024]{1,0:T(8,128)(2,1)} %constant.97.clone.forward_ref, bf16[512,512]{1,0:T(8,128)(2,1)} %constant.98.clone.band_ref, f32[1,512]{1,0:T(1,128)} %constant.99.clone.share_ref), custom_call_target="tpu_custom_call" | custom-call | tf_op jit(solution)/shard_map/pallas_call | solution.py:182
  30.7 1.2 %collective-permute-start.2 = (bf16[1024,128]{1,0:T(8,128)(2,1)}, bf16[1024,128]{1,0:T(8,128)(2,1)S(1)}, u32[]{:S(2)}, u32[]{:S(2)}) collective-permute-start(bf16[1024,128]{1,0:T(8,128)(2,1)} %get-tuple-element.7.p0), channel_id=1, source_target_pairs={{3,0},{0,1},{1,2},{2,3},{7,4},{4,5},{5,6},{6,7},{11,8},{8,9},{9,10... | collective-permute-start | bytes 786440 | tf_op jit(solution)/shard_map/ppermute | solution.py:198
  31.9 2.5 %collective-permute-start.1 = (bf16[1024,128]{1,0:T(8,128)(2,1)}, bf16[1024,128]{1,0:T(8,128)(2,1)S(1)}, u32[]{:S(2)}, u32[]{:S(2)}) collective-permute-start(bf16[1024,128]{1,0:T(8,128)(2,1)} %get-tuple-element.7.p0), channel_id=1, source_target_pairs={{2,0},{3,1},{0,2},{1,3},{6,4},{7,5},{4,6},{5,7},{10,8},{11,9},{8,1... | collective-permute-start | bytes 786440 | tf_op jit(solution)/shard_map/ppermute | solution.py:198
  34.4 1.1 %collective-permute-start = (bf16[1024,128]{1,0:T(8,128)(2,1)}, bf16[1024,128]{1,0:T(8,128)(2,1)S(1)}, u32[]{:S(2)}, u32[]{:S(2)}) collective-permute-start(bf16[1024,128]{1,0:T(8,128)(2,1)} %get-tuple-element.7.p0), channel_id=1, source_target_pairs={{1,0},{2,1},{3,2},{0,3},{5,4},{6,5},{7,6},{4,7},{9,8},{10,9},{11,1... | collective-permute-start | bytes 786440 | tf_op jit(solution)/shard_map/ppermute | solution.py:198
  36.2 0.8 %fusion.3 = s32[8,128,2]{1,2,0:T(2,128)S(1)} fusion(s32[8,128,2]{1,2,0:T(2,128)} %param.9, s32[]{:T(128)S(6)} %axis_index.25, s32[]{:T(128)S(6)} %select_n.39, s32[]{:T(128)S(6)} %sub.28, s32[]{:T(128)S(6)} %axis_index.23), kind=kLoop, calls=%fused_computation.19 | loop fusion | flops 124928 | bytes 16400 | tf_op jit(solution)/shard_map/add | solution.py:205
  37.0 1.4 %collective-permute-start.3 = (bf16[512,128]{1,0:T(8,128)(2,1)}, bf16[512,128]{1,0:T(8,128)(2,1)S(1)}, u32[]{:S(2)}, u32[]{:S(2)}) collective-permute-start(bf16[512,128]{1,0:T(8,128)(2,1)} %get-tuple-element.8), channel_id=1, source_target_pairs={{0,4},{4,0},{8,12},{12,8},{16,20},{20,16},{24,28},{28,24},{32,36},... | collective-permute-start | bytes 393224 | tf_op jit(solution)/shard_map/ppermute | solution.py:196
  38.3 1.2 %collective-permute-done.2.p3 = bf16[1024,128]{1,0:T(8,128)(2,1)S(1)} collective-permute-done((bf16[1024,128]{1,0:T(8,128)(2,1)}, bf16[1024,128]{1,0:T(8,128)(2,1)S(1)}, u32[]{:S(2)}, u32[]{:S(2)}) %collective-permute-start.2) | collective-permute-done | bytes 262176 | tf_op jit(solution)/shard_map/ppermute | solution.py:198
  39.6 1.4 %collective-permute-start.6 = (bf16[512,128]{1,0:T(8,128)(2,1)S(1)}, bf16[512,128]{1,0:T(8,128)(2,1)S(1)}, u32[]{:S(2)}, u32[]{:S(2)}) collective-permute-start(bf16[512,128]{1,0:T(8,128)(2,1)S(1)} %slice.24), channel_id=1, source_target_pairs={{0,4},{4,0},{8,12},{12,8},{16,20},{20,16},{24,28},{28,24},{32,36},... | collective-permute-start | bytes 393224 | tf_op jit(solution)/shard_map/ppermute | solution.py:200
  40.9 5.2 %collective-permute-done.1.p2 = bf16[1024,128]{1,0:T(8,128)(2,1)S(1)} collective-permute-done((bf16[1024,128]{1,0:T(8,128)(2,1)}, bf16[1024,128]{1,0:T(8,128)(2,1)S(1)}, u32[]{:S(2)}, u32[]{:S(2)}) %collective-permute-start.1) | collective-permute-done | bytes 262176 | tf_op jit(solution)/shard_map/ppermute | solution.py:198
  46.2 1.4 %collective-permute-start.5 = (bf16[512,128]{1,0:T(8,128)(2,1)S(1)}, bf16[512,128]{1,0:T(8,128)(2,1)S(1)}, u32[]{:S(2)}, u32[]{:S(2)}) collective-permute-start(bf16[512,128]{1,0:T(8,128)(2,1)S(1)} %slice.23), channel_id=1, source_target_pairs={{0,4},{4,0},{8,12},{12,8},{16,20},{20,16},{24,28},{28,24},{32,36},... | collective-permute-start | bytes 393224 | tf_op jit(solution)/shard_map/ppermute | solution.py:200
  47.6 0.0 collective-permute-done.p1
  47.6 0.1 collective-permute-start.4
  47.7 0.0 collective-permute-done.3.s0
  47.7 0.0 collective-permute-done.6.s3
  47.7 0.8 %collective-permute-done.5.s2 = bf16[512,128]{1,0:T(8,128)(2,1)S(1)} collective-permute-done((bf16[512,128]{1,0:T(8,128)(2,1)S(1)}, bf16[512,128]{1,0:T(8,128)(2,1)S(1)}, u32[]{:S(2)}, u32[]{:S(2)}) %collective-permute-start.5) | collective-permute-done | bytes 131104 | tf_op jit(solution)/shard_map/ppermute | solution.py:200
  48.5 0.5 collective-permute-done.4.s1
  49.0 0.0 copy-done
  49.0 0.0 copy-done.1
  49.0 0.9 %copy-done.2 = bf16[1024,128]{1,0:T(8,128)(2,1)S(1)} copy-done((bf16[1024,128]{1,0:T(8,128)(2,1)S(1)}, bf16[1024,128]{1,0:T(8,128)(2,1)}, u32[]{:S(2)}) %copy-start.2) | copy-done | bytes 262168
  50.0 7.6 %shard_map.84 = f32[1024,1024]{1,0:T(8,128)} custom-call(s32[1]{0:T(128)S(6)} %copy.9.live_ref, s32[1024]{0:T(1024)S(1)} %bitcast.5, bf16[512,512]{1,0:T(8,128)(2,1)S(1)} %copy-done.1, bf16[512,512]{1,0:T(8,128)(2,1)S(1)} %copy-done, bf16[1024,128]{1,0:T(8,128)(2,1)S(1)} %copy-done.2, bf16[1024,128]{1,0:T(8,128)(2,1)S(1)} %collective-permute-done.p1, ...), custom_call_target="tpu_custom_call" | custom-call | tf_op jit(solution)/shard_map/pallas_call | solution.py:209
  (5 shorter events, 0.0 us)
Async XLA Ops:
  0.0 49.0 %copy-start = (bf16[512,512]{1,0:T(8,128)(2,1)S(1)}, bf16[512,512]{1,0:T(8,128)(2,1)}, u32[]{:S(2)}) copy-start(bf16[512,512]{1,0:T(8,128)(2,1)} %constant.101.clone.odd_ref) | copy-start | bytes 1572868
  0.0 49.0 %copy-start.1 = (bf16[512,512]{1,0:T(8,128)(2,1)S(1)}, bf16[512,512]{1,0:T(8,128)(2,1)}, u32[]{:S(2)}) copy-start(bf16[512,512]{1,0:T(8,128)(2,1)} %constant.100.clone.even_ref) | copy-start | bytes 1572868
  30.7 8.9 %collective-permute-start.2 = (bf16[1024,128]{1,0:T(8,128)(2,1)}, bf16[1024,128]{1,0:T(8,128)(2,1)S(1)}, u32[]{:S(2)}, u32[]{:S(2)}) collective-permute-start(bf16[1024,128]{1,0:T(8,128)(2,1)} %get-tuple-element.7.p0), channel_id=1, source_target_pairs={{3,0},{0,1},{1,2},{2,3},{7,4},{4,5},{5,6},{6,7},{11,8},{8,9},{9,10... | collective-permute-start | bytes 786440 | tf_op jit(solution)/shard_map/ppermute | solution.py:198
  31.9 14.3 %collective-permute-start.1 = (bf16[1024,128]{1,0:T(8,128)(2,1)}, bf16[1024,128]{1,0:T(8,128)(2,1)S(1)}, u32[]{:S(2)}, u32[]{:S(2)}) collective-permute-start(bf16[1024,128]{1,0:T(8,128)(2,1)} %get-tuple-element.7.p0), channel_id=1, source_target_pairs={{2,0},{3,1},{0,2},{1,3},{6,4},{7,5},{4,6},{5,7},{10,8},{11,9},{8,1... | collective-permute-start | bytes 786440 | tf_op jit(solution)/shard_map/ppermute | solution.py:198
  34.4 13.2 %collective-permute-start = (bf16[1024,128]{1,0:T(8,128)(2,1)}, bf16[1024,128]{1,0:T(8,128)(2,1)S(1)}, u32[]{:S(2)}, u32[]{:S(2)}) collective-permute-start(bf16[1024,128]{1,0:T(8,128)(2,1)} %get-tuple-element.7.p0), channel_id=1, source_target_pairs={{1,0},{2,1},{3,2},{0,3},{5,4},{6,5},{7,6},{4,7},{9,8},{10,9},{11,1... | collective-permute-start | bytes 786440 | tf_op jit(solution)/shard_map/ppermute | solution.py:198
  37.0 10.7 %collective-permute-start.3 = (bf16[512,128]{1,0:T(8,128)(2,1)}, bf16[512,128]{1,0:T(8,128)(2,1)S(1)}, u32[]{:S(2)}, u32[]{:S(2)}) collective-permute-start(bf16[512,128]{1,0:T(8,128)(2,1)} %get-tuple-element.8), channel_id=1, source_target_pairs={{0,4},{4,0},{8,12},{12,8},{16,20},{20,16},{24,28},{28,24},{32,36},... | collective-permute-start | bytes 393224 | tf_op jit(solution)/shard_map/ppermute | solution.py:196
  39.6 8.1 %collective-permute-start.6 = (bf16[512,128]{1,0:T(8,128)(2,1)S(1)}, bf16[512,128]{1,0:T(8,128)(2,1)S(1)}, u32[]{:S(2)}, u32[]{:S(2)}) collective-permute-start(bf16[512,128]{1,0:T(8,128)(2,1)S(1)} %slice.24), channel_id=1, source_target_pairs={{0,4},{4,0},{8,12},{12,8},{16,20},{20,16},{24,28},{28,24},{32,36},... | collective-permute-start | bytes 393224 | tf_op jit(solution)/shard_map/ppermute | solution.py:200
  46.2 2.4 %collective-permute-start.5 = (bf16[512,128]{1,0:T(8,128)(2,1)S(1)}, bf16[512,128]{1,0:T(8,128)(2,1)S(1)}, u32[]{:S(2)}, u32[]{:S(2)}) collective-permute-start(bf16[512,128]{1,0:T(8,128)(2,1)S(1)} %slice.23), channel_id=1, source_target_pairs={{0,4},{4,0},{8,12},{12,8},{16,20},{20,16},{24,28},{28,24},{32,36},... | collective-permute-start | bytes 393224 | tf_op jit(solution)/shard_map/ppermute | solution.py:200
  47.6 1.4 %collective-permute-start.4 = (bf16[512,128]{1,0:T(8,128)(2,1)S(1)}, bf16[512,128]{1,0:T(8,128)(2,1)S(1)}, u32[]{:S(2)}, u32[]{:S(2)}) collective-permute-start(bf16[512,128]{1,0:T(8,128)(2,1)S(1)} %slice.22), channel_id=1, source_target_pairs={{0,4},{4,0},{8,12},{12,8},{16,20},{20,16},{24,28},{28,24},{32,36},... | collective-permute-start | bytes 393224 | tf_op jit(solution)/shard_map/ppermute | solution.py:200
  49.0 1.0 %copy-start.2 = (bf16[1024,128]{1,0:T(8,128)(2,1)S(1)}, bf16[1024,128]{1,0:T(8,128)(2,1)}, u32[]{:S(2)}) copy-start(bf16[1024,128]{1,0:T(8,128)(2,1)} %get-tuple-element.7.p0) | copy-start | bytes 786436

commit v2 on v1

--- a/solution.py
+++ b/solution.py
@@ -57,7 +57,9 @@
         out_ref[block * LANES : (block + 1) * LANES, :] = part.T.astype(jnp.bfloat16)
 
 
-def whiten_kernel(parts_ref, forward_ref, band_ref, share_ref, both_ref, given_ref, segs, wide):
+def whiten_kernel(
+    parts_ref, forward_ref, band_ref, share_ref, both_ref, given_ref, other_ref, segs, wide
+):
     core = lax.rem(lax.axis_index("sta"), 2)
     low = lax.broadcasted_iota(jnp.int32, (PER, LANES), 1) < LANES // 2
     for e in range(SEGMENTS):
@@ -104,10 +106,11 @@
     both_ref[:size, :] = given_rows
     both_ref[size:, :] = other_rows
     given_ref[...] = given_rows
+    other_ref[...] = other_rows
 
 
 def pair_kernel(
-    live_ref, index_ref, even_ref, odd_ref, p0, p1, p2, p3, s0, s1, s2, s3, out_ref, table, mixed
+    live_ref, index_ref, even_ref, odd_ref, b0, b1, g2, o2, b3, s0, s1, s2, s3, out_ref, table, mixed
 ):
     step = pl.program_id(0)
     size = PER * ROWS
@@ -115,14 +118,20 @@
 
     @pl.when(step == 0)
     def _():
-        for net, (pieces, swapped) in enumerate(((p0, s0), (p1, s1), (p2, s2), (p3, s3))):
+        sources = (
+            ((b0, 0), (b0, size), (s0, 0)),
+            ((b1, 0), (b1, size), (s1, 0)),
+            ((g2, 0), (o2, 0), (s2, 0)),
+            ((b3, 0), (b3, size), (s3, 0)),
+        )
+        for net in range(NETS):
             for slot in range(SLOTS):
-                source = swapped if slot == 2 else pieces
-                start = 0 if slot == 2 else slot * size
+                source, start = sources[net][slot]
                 for k in range(PER):
-                    table[(slot * NETS + net) * PER + k] = source[
-                        start + k * ROWS : start + (k + 1) * ROWS, :
-                    ].astype(jnp.float32)
+                    at = start + k * ROWS
+                    table[(slot * NETS + net) * PER + k] = source[at : at + ROWS, :].astype(
+                        jnp.float32
+                    )
 
     upper = lax.broadcasted_iota(jnp.int32, (8, LANES), 0) < 4
 
@@ -140,11 +149,11 @@
         mixed[pl.ds(pl.multiple_of(q * 8, 8), 8), :] = jnp.where(upper, real, imag) + turned
 
     def some(g, carry):
-        for q in range(8):
-            mix(g * 8 + q)
+        for q in range(32):
+            mix(g * 32 + q)
         return carry
 
-    lax.fori_loop(0, STEP_PAIRS // 8, some, 0)
+    lax.fori_loop(0, STEP_PAIRS // 32, some, 0)
 
     def rows_of(blocks):
         return jnp.concatenate(
@@ -173,31 +182,40 @@
         out_shape=jax.ShapeDtypeStruct((columns * PER, LANES), jnp.bfloat16),
         in_specs=[vmem],
         out_specs=vmem,
+        compiler_params=pltpu.CompilerParams(vmem_limit_bytes=8 * 2**20),
+        cost_estimate=pl.CostEstimate(flops=2 * 10**10, bytes_accessed=3 * 2**17, transcendentals=0),
     )(records.T)
     received = lax.all_to_all(
         messages.reshape(columns, PER, LANES), "sta", split_axis=0, concat_axis=0, tiled=True
     ).reshape(columns * PER, LANES)
     band, share = band_tables()
     size = PER * ROWS
-    both, given = pl.pallas_call(
+    both, given, other = pl.pallas_call(
         whiten_kernel,
         out_shape=(
             jax.ShapeDtypeStruct((2 * size, LANES), jnp.bfloat16),
             jax.ShapeDtypeStruct((size, LANES), jnp.bfloat16),
+            jax.ShapeDtypeStruct((size, LANES), jnp.bfloat16),
         ),
         in_specs=[vmem] * 4,
-        out_specs=(vmem, vmem),
+        out_specs=(vmem, vmem, vmem),
         scratch_shapes=[
             pltpu.VMEM((2 * SEGMENTS * PER, POINTS), jnp.bfloat16),
             pltpu.VMEM((2 * size, LANES), jnp.float32),
         ],
+        compiler_params=pltpu.CompilerParams(vmem_limit_bytes=16 * 2**20),
+        cost_estimate=pl.CostEstimate(flops=2 * 10**9, bytes_accessed=3 * 2**20, transcendentals=0),
     )(received, jnp.asarray(forward_table()), jnp.asarray(band), jnp.asarray(share))
-    swap = [(i, i ^ 1) for i in range(columns)]
-    pieces, swapped = [both], [lax.ppermute(given, "sta", swap)]
-    for by in range(1, nets):
-        piece = lax.ppermute(both, "grp", [((i + by) % nets, i) for i in range(nets)])
-        pieces.append(piece)
-        swapped.append(lax.ppermute(piece[:size], "sta", swap))
+    def from_net(value, by):
+        return lax.ppermute(value, "grp", [((i + by) % nets, i) for i in range(nets)])
+
+    def from_other_core(value):
+        return lax.ppermute(value, "sta", [(i, i ^ 1) for i in range(columns)])
+
+    other2, given2 = from_net(other, 2), from_net(given, 2)
+    both1, both3 = from_net(both, 1), from_net(both, 3)
+    pieces = [both, both1, given2, other2, both3]
+    swapped = [from_other_core(part) for part in (given, both1[:size], given2, both3[:size])]
 
     station_net = pair_list // (columns * PER)
     offset = pair_list // PER % columns - column
@@ -210,13 +228,14 @@
         pair_kernel,
         grid=(pairs // STEP_PAIRS,),
         out_shape=jax.ShapeDtypeStruct((pairs, POINTS), jnp.float32),
-        in_specs=[smem, smem] + [vmem] * 10,
+        in_specs=[smem, smem] + [vmem] * 11,
         out_specs=pl.BlockSpec((STEP_PAIRS, POINTS), lambda i: (i, 0)),
         scratch_shapes=[
             pltpu.VMEM((SLOTS * NETS * PER, ROWS, LANES), jnp.float32),
             pltpu.VMEM((STEP_PAIRS * 8, LANES), jnp.float32),
         ],
-        compiler_params=pltpu.CompilerParams(vmem_limit_bytes=40 * 2**20),
+        compiler_params=pltpu.CompilerParams(vmem_limit_bytes=24 * 2**20),
+        cost_estimate=pl.CostEstimate(flops=6 * 10**9, bytes_accessed=6 * 2**20, transcendentals=0),
     )(live_blocks, index, jnp.asarray(even), jnp.asarray(odd), *pieces, *swapped).reshape(
         pair_list.shape[0], BLOCK, POINTS
     )

time: 57.8 us -> 50.5 us (0.87)
  the two profiles are of different devices: /device:TPU:1 before, /device:TPU:6 now
where the time goes in v2:
time: 50.5 us; the launch traced here: 49.8 us
  blocking collectives  24.2 us (48%)
  waiting for transfers between devices  9.4 us (19%)
  Pallas kernels  7.79 us (15%)
  starting transfers between devices  6.59 us (13%)
  local copies, waits for them, and re-layouts  0.95 us (2%)
  between operations  0.77 us (2%)
    all_to_all x1, blocking collectives, local(): lax.all_to_all(messages.reshape(columns, PER, LANES), 'sta', split_axis=0...  24.2 us
    ppermute x4, waiting for transfers between devices, from_net(): lax.ppermute(value, 'grp', [((i + by) % nets, i) for i in range(nets)])  8.12 us
    pallas_call x1, Pallas kernels, local(): pl.pallas_call(pair_kernel, grid=(pairs // STEP_PAIRS,), out_shape=jax.Sh...  6.55 us
    ppermute x4, starting transfers between devices, from_net(): lax.ppermute(value, 'grp', [((i + by) % nets, i) for i in range(nets)])  5.81 us
    ppermute x4, waiting for transfers between devices, from_other_core(): return lax.ppermute(value, 'sta', [(i, i ^ 1) for i in range(columns)])  1.28 us
    pallas_call x1, Pallas kernels, local(): pl.pallas_call(whiten_kernel, out_shape=(jax.ShapeDtypeStruct((2 * size,...  1.04 us
  transfers between devices with their start and end apart: 8, of which 3 were waited for; matrix products, arithmetic and copies ran while one was open for 0% of the time, Pallas kernels for 0%

profile of v2, /device:TPU:6, one launch (start us, length us, event | category | flops | bytes accessed | tf_op | source)
XLA Modules:
  0.0 49.8 jit_solution(17096083380525446272)
XLA Ops:
  0.0 0.9 %copy-done = bf16[1024,64]{0,1:T(8,128)(2,1)S(1)} copy-done((bf16[1024,64]{0,1:T(8,128)(2,1)S(1)}, bf16[1024,64]{0,1:T(8,128)(2,1)}, u32[]{:S(2)}) %copy-start) | copy-done | bytes 131096
  0.9 0.2 shard_map.82
  1.1 0.0 copy-start.6
  1.1 0.0 copy-start.2
  1.1 0.0 copy-start.3
  1.2 24.2 %all_to_all.5 = bf16[64,16,128]{2,1,0:T(8,128)(2,1)S(1)} all-to-all(bf16[64,16,128]{2,1,0:T(8,128)(2,1)S(1)} %bitcast.6), channel_id=1, replica_groups=mesh['sta'=64,'grp'=4] {'sta'}, dimensions={0} | all-to-all | bytes 524288 | tf_op jit(solution)/shard_map/all_to_all | solution.py:188
  25.3 1.0 %shard_map.83 = (bf16[1024,128]{1,0:T(8,128)(2,1)S(1)}, bf16[512,128]{1,0:T(8,128)(2,1)S(1)}, bf16[512,128]{1,0:T(8,128)(2,1)S(1)}) custom-call(bf16[1024,128]{1,0:T(8,128)(2,1)S(1)} %bitcast.5, bf16[1024,1024]{1,0:T(8,128)(2,1)S(1)} %copy-done.1, bf16[512,512]{1,0:T(8,128)(2,1)S(1)} %copy-done.4, f32[1,512]{1,0:T(1,128)S(1)} %copy-done.5), custom_call_target="tpu_custom_call" | custom-call | flops 2000000000 | bytes 3145728 | tf_op jit(solution)/shard_map/pallas_call | solution.py:193
  26.4 0.6 %collective-permute-start.3 = (bf16[1024,128]{1,0:T(8,128)(2,1)S(1)}, bf16[1024,128]{1,0:T(8,128)(2,1)S(1)}, u32[]{:S(2)}, u32[]{:S(2)}) collective-permute-start(bf16[1024,128]{1,0:T(8,128)(2,1)S(1)} %get-tuple-element.8.b0), channel_id=1, source_target_pairs={{3,0},{0,1},{1,2},{2,3},{7,4},{4,5},{5,6},{6,7},{11,8},{8,9},{9,10... | collective-permute-start | bytes 786440 | tf_op jit(solution)/shard_map/ppermute | solution.py:210
  26.9 1.5 %collective-permute-start = (bf16[1024,128]{1,0:T(8,128)(2,1)S(1)}, bf16[1024,128]{1,0:T(8,128)(2,1)S(1)}, u32[]{:S(2)}, u32[]{:S(2)}) collective-permute-start(bf16[1024,128]{1,0:T(8,128)(2,1)S(1)} %get-tuple-element.8.b0), channel_id=1, source_target_pairs={{1,0},{2,1},{3,2},{0,3},{5,4},{6,5},{7,6},{4,7},{9,8},{10,9},{11,1... | collective-permute-start | bytes 786440 | tf_op jit(solution)/shard_map/ppermute | solution.py:210
  29.1 1.5 %collective-permute-start.1 = (bf16[512,128]{1,0:T(8,128)(2,1)S(1)}, bf16[512,128]{1,0:T(8,128)(2,1)S(1)}, u32[]{:S(2)}, u32[]{:S(2)}) collective-permute-start(bf16[512,128]{1,0:T(8,128)(2,1)S(1)} %get-tuple-element.9), channel_id=1, source_target_pairs={{2,0},{3,1},{0,2},{1,3},{6,4},{7,5},{4,6},{5,7},{10,8},{11,9},{8,1... | collective-permute-start | bytes 393224 | tf_op jit(solution)/shard_map/ppermute | solution.py:210
  30.6 0.1 fusion.3
  30.7 0.1 collective-permute-start.4
  30.8 2.2 %collective-permute-start.2 = (bf16[512,128]{1,0:T(8,128)(2,1)S(1)}, bf16[512,128]{1,0:T(8,128)(2,1)S(1)}, u32[]{:S(2)}, u32[]{:S(2)}) collective-permute-start(bf16[512,128]{1,0:T(8,128)(2,1)S(1)} %get-tuple-element.10), channel_id=1, source_target_pairs={{2,0},{3,1},{0,2},{1,3},{6,4},{7,5},{4,6},{5,7},{10,8},{11,9},{8,1... | collective-permute-start | bytes 393224 | tf_op jit(solution)/shard_map/ppermute | solution.py:210
  33.0 7.0 %collective-permute-done.1.g2 = bf16[512,128]{1,0:T(8,128)(2,1)S(1)} collective-permute-done((bf16[512,128]{1,0:T(8,128)(2,1)S(1)}, bf16[512,128]{1,0:T(8,128)(2,1)S(1)}, u32[]{:S(2)}, u32[]{:S(2)}) %collective-permute-start.1) | collective-permute-done | bytes 131104 | tf_op jit(solution)/shard_map/ppermute | solution.py:210
  40.0 0.0 collective-permute-start.6
  40.0 0.0 collective-permute-done.3.b3
  40.0 0.6 %collective-permute-start.7 = (bf16[512,128]{1,0:T(8,128)(2,1)S(1)}, bf16[512,128]{1,0:T(8,128)(2,1)S(1)}, u32[]{:S(2)}, u32[]{:S(2)}) collective-permute-start(bf16[512,128]{1,0:T(8,128)(2,1)S(1)} %slice.19), channel_id=1, source_target_pairs={{0,4},{4,0},{8,12},{12,8},{16,20},{20,16},{24,28},{28,24},{32,36},... | collective-permute-start | bytes 393224 | tf_op jit(solution)/shard_map/ppermute | solution.py:213
  40.6 1.2 %collective-permute-done.b1 = bf16[1024,128]{1,0:T(8,128)(2,1)S(1)} collective-permute-done((bf16[1024,128]{1,0:T(8,128)(2,1)S(1)}, bf16[1024,128]{1,0:T(8,128)(2,1)S(1)}, u32[]{:S(2)}, u32[]{:S(2)}) %collective-permute-start) | collective-permute-done | bytes 262176 | tf_op jit(solution)/shard_map/ppermute | solution.py:210
  41.8 0.1 collective-permute-start.5
  41.9 0.0 collective-permute-done.2.o2
  41.9 0.0 collective-permute-done.6.s2
  41.9 0.0 collective-permute-done.7.s3
  41.9 1.3 %collective-permute-done.5.s1 = bf16[512,128]{1,0:T(8,128)(2,1)S(1)} collective-permute-done((bf16[512,128]{1,0:T(8,128)(2,1)S(1)}, bf16[512,128]{1,0:T(8,128)(2,1)S(1)}, u32[]{:S(2)}, u32[]{:S(2)}) %collective-permute-start.5) | collective-permute-done | bytes 131104 | tf_op jit(solution)/shard_map/ppermute | solution.py:213
  43.2 6.5 %shard_map.84 = f32[1024,1024]{1,0:T(8,128)} custom-call(s32[1]{0:T(128)S(6)} %copy.9.live_ref, s32[1024]{0:T(1024)S(1)} %bitcast.7, bf16[512,512]{1,0:T(8,128)(2,1)S(1)} %copy-done.3, bf16[512,512]{1,0:T(8,128)(2,1)S(1)} %copy-done.2, bf16[1024,128]{1,0:T(8,128)(2,1)S(1)} %get-tuple-element.8.b0, bf16[1024,128]{1,0:T(8,128)(2,1)S(1)} %collective-permute-done.b1, ...), custom_call_target="tpu_custom_call" | custom-call | flops 6000000000 | bytes 6291456 | tf_op jit(solution)/shard_map/pallas_call | solution.py:227
  (14 shorter events, 0.0 us)
Async XLA Ops:
  0.0 0.9 %copy-start = (bf16[1024,64]{0,1:T(8,128)(2,1)S(1)}, bf16[1024,64]{0,1:T(8,128)(2,1)}, u32[]{:S(2)}) copy-start(bf16[1024,64]{0,1:T(8,128)(2,1)} %param.8) | copy-start | bytes 393220
  0.9 24.4 %copy-start.1 = (bf16[1024,1024]{1,0:T(8,128)(2,1)S(1)}, bf16[1024,1024]{1,0:T(8,128)(2,1)}, u32[]{:S(2)}) copy-start(bf16[1024,1024]{1,0:T(8,128)(2,1)} %constant.97.clone.forward_ref) | copy-start | bytes 6291460
  0.9 24.4 %copy-start.4 = (bf16[512,512]{1,0:T(8,128)(2,1)S(1)}, bf16[512,512]{1,0:T(8,128)(2,1)}, u32[]{:S(2)}) copy-start(bf16[512,512]{1,0:T(8,128)(2,1)} %constant.98.clone.band_ref) | copy-start | bytes 1572868
  0.9 24.4 %copy-start.5 = (f32[1,512]{1,0:T(1,128)S(1)}, f32[1,512]{1,0:T(1,128)}, u32[]{:S(2)}) copy-start(f32[1,512]{1,0:T(1,128)} %constant.99.clone.share_ref) | copy-start | bytes 6148
  1.1 29.5 %copy-start.6 = (s32[8,128,2]{1,2,0:T(2,128)S(1)}, s32[8,128,2]{1,2,0:T(2,128)}, u32[]{:S(2)}) copy-start(s32[8,128,2]{1,2,0:T(2,128)} %param.9) | copy-start | bytes 24580
  1.1 42.1 %copy-start.2 = (bf16[512,512]{1,0:T(8,128)(2,1)S(1)}, bf16[512,512]{1,0:T(8,128)(2,1)}, u32[]{:S(2)}) copy-start(bf16[512,512]{1,0:T(8,128)(2,1)} %constant.101.clone.odd_ref) | copy-start | bytes 1572868
  1.1 42.1 %copy-start.3 = (bf16[512,512]{1,0:T(8,128)(2,1)S(1)}, bf16[512,512]{1,0:T(8,128)(2,1)}, u32[]{:S(2)}) copy-start(bf16[512,512]{1,0:T(8,128)(2,1)} %constant.100.clone.even_ref) | copy-start | bytes 1572868
  26.4 13.6 %collective-permute-start.3 = (bf16[1024,128]{1,0:T(8,128)(2,1)S(1)}, bf16[1024,128]{1,0:T(8,128)(2,1)S(1)}, u32[]{:S(2)}, u32[]{:S(2)}) collective-permute-start(bf16[1024,128]{1,0:T(8,128)(2,1)S(1)} %get-tuple-element.8.b0), channel_id=1, source_target_pairs={{3,0},{0,1},{1,2},{2,3},{7,4},{4,5},{5,6},{6,7},{11,8},{8,9},{9,10... | collective-permute-start | bytes 786440 | tf_op jit(solution)/shard_map/ppermute | solution.py:210
  26.9 14.8 %collective-permute-start = (bf16[1024,128]{1,0:T(8,128)(2,1)S(1)}, bf16[1024,128]{1,0:T(8,128)(2,1)S(1)}, u32[]{:S(2)}, u32[]{:S(2)}) collective-permute-start(bf16[1024,128]{1,0:T(8,128)(2,1)S(1)} %get-tuple-element.8.b0), channel_id=1, source_target_pairs={{1,0},{2,1},{3,2},{0,3},{5,4},{6,5},{7,6},{4,7},{9,8},{10,9},{11,1... | collective-permute-start | bytes 786440 | tf_op jit(solution)/shard_map/ppermute | solution.py:210
  29.1 10.8 %collective-permute-start.1 = (bf16[512,128]{1,0:T(8,128)(2,1)S(1)}, bf16[512,128]{1,0:T(8,128)(2,1)S(1)}, u32[]{:S(2)}, u32[]{:S(2)}) collective-permute-start(bf16[512,128]{1,0:T(8,128)(2,1)S(1)} %get-tuple-element.9), channel_id=1, source_target_pairs={{2,0},{3,1},{0,2},{1,3},{6,4},{7,5},{4,6},{5,7},{10,8},{11,9},{8,1... | collective-permute-start | bytes 393224 | tf_op jit(solution)/shard_map/ppermute | solution.py:210
  30.7 11.2 %collective-permute-start.4 = (bf16[512,128]{1,0:T(8,128)(2,1)S(1)}, bf16[512,128]{1,0:T(8,128)(2,1)S(1)}, u32[]{:S(2)}, u32[]{:S(2)}) collective-permute-start(bf16[512,128]{1,0:T(8,128)(2,1)S(1)} %get-tuple-element.9), channel_id=1, source_target_pairs={{0,4},{4,0},{8,12},{12,8},{16,20},{20,16},{24,28},{28,24},{32,36},... | collective-permute-start | bytes 393224 | tf_op jit(solution)/shard_map/ppermute | solution.py:213
  30.8 11.1 %collective-permute-start.2 = (bf16[512,128]{1,0:T(8,128)(2,1)S(1)}, bf16[512,128]{1,0:T(8,128)(2,1)S(1)}, u32[]{:S(2)}, u32[]{:S(2)}) collective-permute-start(bf16[512,128]{1,0:T(8,128)(2,1)S(1)} %get-tuple-element.10), channel_id=1, source_target_pairs={{2,0},{3,1},{0,2},{1,3},{6,4},{7,5},{4,6},{5,7},{10,8},{11,9},{8,1... | collective-permute-start | bytes 393224 | tf_op jit(solution)/shard_map/ppermute | solution.py:210
  40.0 1.9 %collective-permute-start.6 = (bf16[512,128]{1,0:T(8,128)(2,1)S(1)}, bf16[512,128]{1,0:T(8,128)(2,1)S(1)}, u32[]{:S(2)}, u32[]{:S(2)}) collective-permute-start(bf16[512,128]{1,0:T(8,128)(2,1)S(1)} %collective-permute-done.1.g2), channel_id=1, source_target_pairs={{0,4},{4,0},{8,12},{12,8},{16,20},{20,16},{24,28},{28,24},{32,36},... | collective-permute-start | bytes 393224 | tf_op jit(solution)/shard_map/ppermute | solution.py:213
  40.0 1.9 %collective-permute-start.7 = (bf16[512,128]{1,0:T(8,128)(2,1)S(1)}, bf16[512,128]{1,0:T(8,128)(2,1)S(1)}, u32[]{:S(2)}, u32[]{:S(2)}) collective-permute-start(bf16[512,128]{1,0:T(8,128)(2,1)S(1)} %slice.19), channel_id=1, source_target_pairs={{0,4},{4,0},{8,12},{12,8},{16,20},{20,16},{24,28},{28,24},{32,36},... | collective-permute-start | bytes 393224 | tf_op jit(solution)/shard_map/ppermute | solution.py:213
  41.8 1.4 %collective-permute-start.5 = (bf16[512,128]{1,0:T(8,128)(2,1)S(1)}, bf16[512,128]{1,0:T(8,128)(2,1)S(1)}, u32[]{:S(2)}, u32[]{:S(2)}) collective-permute-start(bf16[512,128]{1,0:T(8,128)(2,1)S(1)} %slice.18), channel_id=1, source_target_pairs={{0,4},{4,0},{8,12},{12,8},{16,20},{20,16},{24,28},{28,24},{32,36},... | collective-permute-start | bytes 393224 | tf_op jit(solution)/shard_map/ppermute | solution.py:213

commit v3 on v2

--- a/solution.py
+++ b/solution.py
@@ -20,6 +20,8 @@
 ROWS = 32
 LANES = 128
 STEP_PAIRS = 256
+UNROLL = 64
+ZERO_ROW = SLOTS * NETS * PER * ROWS
 
 BIN_ORDER = np.concatenate([np.arange(2, BINS + 1, 2), np.arange(1, BINS + 1, 2)])
 
@@ -110,63 +112,72 @@
 
 
 def pair_kernel(
-    live_ref, index_ref, even_ref, odd_ref, b0, b1, g2, o2, b3, s0, s1, s2, s3, out_ref, table, mixed
+    index_ref, even_ref, odd_ref, b0, b1, g2, o2, b3, s0, s1, s2, s3, out_ref, *scratch
 ):
-    step = pl.program_id(0)
+    table, reals, imags, result, places, place_sem, sems = scratch
     size = PER * ROWS
     half = ROWS // 4
-
-    @pl.when(step == 0)
-    def _():
-        sources = (
-            ((b0, 0), (b0, size), (s0, 0)),
-            ((b1, 0), (b1, size), (s1, 0)),
-            ((g2, 0), (o2, 0), (s2, 0)),
-            ((b3, 0), (b3, size), (s3, 0)),
-        )
-        for net in range(NETS):
-            for slot in range(SLOTS):
-                source, start = sources[net][slot]
-                for k in range(PER):
-                    at = start + k * ROWS
-                    table[(slot * NETS + net) * PER + k] = source[at : at + ROWS, :].astype(
-                        jnp.float32
-                    )
-
-    upper = lax.broadcasted_iota(jnp.int32, (8, LANES), 0) < 4
-
-    def mix(q):
-        packed = index_ref[step * STEP_PAIRS + q]
-        i = packed & 255
-        j = packed >> 8
-        ar0, ar1 = table[i, 0:half], table[i, half : 2 * half]
-        ai0, ai1 = table[i, 2 * half : 3 * half], table[i, 3 * half : 4 * half]
-        br0, br1 = table[j, 0:half], table[j, half : 2 * half]
-        bi0, bi1 = table[j, 2 * half : 3 * half], table[j, 3 * half : 4 * half]
-        real = (ar0 * br0 + ar1 * br1) + (ai0 * bi0 + ai1 * bi1)
-        imag = (ai0 * br0 + ai1 * br1) - (ar0 * bi0 + ar1 * bi1)
-        turned = pltpu.roll(jnp.where(upper, imag, real), 4, 0)
-        mixed[pl.ds(pl.multiple_of(q * 8, 8), 8), :] = jnp.where(upper, real, imag) + turned
-
-    def some(g, carry):
-        for q in range(32):
-            mix(g * 32 + q)
+    pairs = index_ref.shape[0] // 2
+    load_places = pltpu.make_async_copy(index_ref, places, place_sem)
+    load_places.start()
+    sources = (
+        ((b0, 0), (b0, size), (s0, 0)),
+        ((b1, 0), (b1, size), (s1, 0)),
+        ((g2, 0), (o2, 0), (s2, 0)),
+        ((b3, 0), (b3, size), (s3, 0)),
+    )
+    for net in range(NETS):
+        for slot in range(SLOTS):
+            source, start = sources[net][slot]
+            row = (slot * NETS + net) * size
+            table[row : row + size, :] = source[start : start + size, :].astype(jnp.float32)
+    table[ZERO_ROW : ZERO_ROW + ROWS, :] = jnp.zeros((ROWS, LANES), jnp.float32)
+    load_places.wait()
+
+    def mix(step, q):
+        at = step * STEP_PAIRS + q
+        first = table[pl.ds(pl.multiple_of(places[at], ROWS), ROWS), :]
+        second = table[pl.ds(pl.multiple_of(places[pairs + at], ROWS), ROWS), :]
+        ar0, ar1, ai0, ai1 = (first[n : n + half] for n in range(0, ROWS, half))
+        br0, br1, bi0, bi1 = (second[n : n + half] for n in range(0, ROWS, half))
+        rows = pl.ds(pl.multiple_of(q * half, half), half)
+        reals[rows, :] = (ar0 * br0 + ar1 * br1) + (ai0 * bi0 + ai1 * bi1)
+        imags[rows, :] = (ai0 * br0 + ai1 * br1) - (ar0 * bi0 + ar1 * bi1)
+
+    def rows_of(first_block):
+        blocks = []
+        for part in (reals, imags):
+            for b in (first_block, first_block + 1):
+                low = part[pl.ds(b, STEP_PAIRS, stride=half), :]
+                high = part[pl.ds(b + half // 2, STEP_PAIRS, stride=half), :]
+                blocks.append((low + high).astype(jnp.bfloat16))
+        return jnp.concatenate(blocks, axis=1)
+
+    def send(step):
+        rows = pl.ds(pl.multiple_of(step * STEP_PAIRS, STEP_PAIRS), STEP_PAIRS)
+        return pltpu.make_async_copy(result.at[rows], out_ref.at[rows], sems.at[step])
+
+    def run(step, carry):
+        def some(g, inner):
+            for q in range(UNROLL):
+                mix(step, g * UNROLL + q)
+            return inner
+
+        lax.fori_loop(0, STEP_PAIRS // UNROLL, some, 0)
+        even = jnp.dot(rows_of(0), even_ref[...], preferred_element_type=jnp.float32)
+        odd = jnp.dot(rows_of(2), odd_ref[...], preferred_element_type=jnp.float32)
+        here = pl.ds(pl.multiple_of(step * STEP_PAIRS, STEP_PAIRS), STEP_PAIRS)
+        result[here, : POINTS // 2] = even + odd
+        result[here, POINTS // 2 :] = even - odd
+        send(step).start()
         return carry
 
-    lax.fori_loop(0, STEP_PAIRS // 32, some, 0)
-
-    def rows_of(blocks):
-        return jnp.concatenate(
-            [mixed[pl.ds(b, STEP_PAIRS, stride=8), :].astype(jnp.bfloat16) for b in blocks], axis=1
-        )
-
-    even = jnp.dot(rows_of((0, 1, 4, 5)), even_ref[...], preferred_element_type=jnp.float32)
-    odd = jnp.dot(rows_of((2, 3, 6, 7)), odd_ref[...], preferred_element_type=jnp.float32)
-    for b in range(STEP_PAIRS // BLOCK):
-        keep = (step * (STEP_PAIRS // BLOCK) + b < live_ref[0]).astype(jnp.float32)
-        here = slice(b * BLOCK, (b + 1) * BLOCK)
-        out_ref[here, : POINTS // 2] = (even[here] + odd[here]) * keep
-        out_ref[here, POINTS // 2 :] = (even[here] - odd[here]) * keep
+    def finish(step, carry):
+        send(step).wait()
+        return carry
+
+    lax.fori_loop(0, pairs // STEP_PAIRS, run, 0)
+    lax.fori_loop(0, pairs // STEP_PAIRS, finish, 0)
 
 
 def local(records, pair_list, live_blocks):
@@ -176,7 +187,6 @@
     net = lax.axis_index("grp")
     core = column % 2
     vmem = pl.BlockSpec(memory_space=pltpu.VMEM)
-    smem = pl.BlockSpec(memory_space=pltpu.SMEM)
     messages = pl.pallas_call(
         pack_kernel,
         out_shape=jax.ShapeDtypeStruct((columns * PER, LANES), jnp.bfloat16),
@@ -220,23 +230,29 @@
     station_net = pair_list // (columns * PER)
     offset = pair_list // PER % columns - column
     slot = jnp.where(offset == 1, 2, jnp.where(offset == 0, 1 - core, core))
-    place = (slot * nets + (station_net - net) % nets) * PER + pair_list % PER
-    index = (place[:, :, 0] + 256 * place[:, :, 1]).reshape(-1)
+    place = ((slot * nets + (station_net - net) % nets) * PER + pair_list % PER) * ROWS
+    in_use = jnp.arange(pair_list.shape[0], dtype=jnp.int32)[:, None, None] < live_blocks[0]
+    index = jnp.where(in_use, place, ZERO_ROW).transpose(2, 0, 1).reshape(-1)
     even, odd = lag_tables()
-    pairs = index.shape[0]
+    pairs = pair_list.shape[0] * BLOCK
+    steps = pairs // STEP_PAIRS
     return pl.pallas_call(
         pair_kernel,
-        grid=(pairs // STEP_PAIRS,),
         out_shape=jax.ShapeDtypeStruct((pairs, POINTS), jnp.float32),
-        in_specs=[smem, smem] + [vmem] * 11,
-        out_specs=pl.BlockSpec((STEP_PAIRS, POINTS), lambda i: (i, 0)),
+        in_specs=[vmem] * 12,
+        out_specs=pl.BlockSpec(memory_space=pl.ANY),
         scratch_shapes=[
-            pltpu.VMEM((SLOTS * NETS * PER, ROWS, LANES), jnp.float32),
-            pltpu.VMEM((STEP_PAIRS * 8, LANES), jnp.float32),
+            pltpu.VMEM((ZERO_ROW + ROWS, LANES), jnp.float32),
+            pltpu.VMEM((STEP_PAIRS * ROWS // 4, LANES), jnp.float32),
+            pltpu.VMEM((STEP_PAIRS * ROWS // 4, LANES), jnp.float32),
+            pltpu.VMEM((pairs, POINTS), jnp.float32),
+            pltpu.SMEM((2 * pairs,), jnp.int32),
+            pltpu.SemaphoreType.DMA,
+            pltpu.SemaphoreType.DMA((steps,)),
         ],
         compiler_params=pltpu.CompilerParams(vmem_limit_bytes=24 * 2**20),
         cost_estimate=pl.CostEstimate(flops=6 * 10**9, bytes_accessed=6 * 2**20, transcendentals=0),
-    )(live_blocks, index, jnp.asarray(even), jnp.asarray(odd), *pieces, *swapped).reshape(
+    )(index, jnp.asarray(even), jnp.asarray(odd), *pieces, *swapped).reshape(
         pair_list.shape[0], BLOCK, POINTS
     )
 

time: 50.5 us -> 49.6 us (0.982)
  Pallas kernels: 7.79 us -> 6.9 us
    pallas_call x1, Pallas kernels: 6.55 us -> 5.66 us  [local(): pl.pallas_call(pair_kernel, out_shape=jax.ShapeDtypeStruct((pairs, POINTS...]
where the time goes in v3:
time: 49.6 us; the launch traced here: 48.9 us
  blocking collectives  24.2 us (49%)
  waiting for transfers between devices  9.51 us (19%)
  Pallas kernels  6.9 us (14%)
  starting transfers between devices  6.5 us (13%)
  local copies, waits for them, and re-layouts  0.95 us (2%)
  between operations  0.76 us (2%)
    all_to_all x1, blocking collectives, local(): lax.all_to_all(messages.reshape(columns, PER, LANES), 'sta', split_axis=0...  24.2 us
    ppermute x4, waiting for transfers between devices, from_net(): lax.ppermute(value, 'grp', [((i + by) % nets, i) for i in range(nets)])  8.28 us
    ppermute x4, starting transfers between devices, from_net(): lax.ppermute(value, 'grp', [((i + by) % nets, i) for i in range(nets)])  5.72 us
    pallas_call x1, Pallas kernels, local(): pl.pallas_call(pair_kernel, out_shape=jax.ShapeDtypeStruct((pairs, POINTS...  5.66 us
    ppermute x4, waiting for transfers between devices, from_other_core(): return lax.ppermute(value, 'sta', [(i, i ^ 1) for i in range(columns)])  1.23 us
    pallas_call x1, Pallas kernels, local(): pl.pallas_call(whiten_kernel, out_shape=(jax.ShapeDtypeStruct((2 * size,...  1.04 us
  transfers between devices with their start and end apart: 8, of which 3 were waited for; matrix products, arithmetic and copies ran while one was open for 0% of the time, Pallas kernels for 0%

profile of v3, /device:TPU:6, one launch (start us, length us, event | category | flops | bytes accessed | tf_op | source)
XLA Modules:
  0.0 48.9 jit_solution(16931106625113043069)
XLA Ops:
  0.0 0.9 %copy-done = bf16[1024,64]{0,1:T(8,128)(2,1)S(1)} copy-done((bf16[1024,64]{0,1:T(8,128)(2,1)S(1)}, bf16[1024,64]{0,1:T(8,128)(2,1)}, u32[]{:S(2)}) %copy-start) | copy-done | bytes 131096
  0.9 0.2 shard_map.82
  1.1 0.0 copy-start.6
  1.1 0.0 copy-start.2
  1.1 0.0 copy-start.3
  1.2 24.2 %all_to_all.5 = bf16[64,16,128]{2,1,0:T(8,128)(2,1)S(1)} all-to-all(bf16[64,16,128]{2,1,0:T(8,128)(2,1)S(1)} %bitcast.11), channel_id=1, replica_groups=mesh['sta'=64,'grp'=4] {'sta'}, dimensions={0} | all-to-all | bytes 524288 | tf_op jit(solution)/shard_map/all_to_all | solution.py:198
  25.3 1.0 %shard_map.83 = (bf16[1024,128]{1,0:T(8,128)(2,1)S(1)}, bf16[512,128]{1,0:T(8,128)(2,1)S(1)}, bf16[512,128]{1,0:T(8,128)(2,1)S(1)}) custom-call(bf16[1024,128]{1,0:T(8,128)(2,1)S(1)} %bitcast.10, bf16[1024,1024]{1,0:T(8,128)(2,1)S(1)} %copy-done.1, bf16[512,512]{1,0:T(8,128)(2,1)S(1)} %copy-done.4, f32[1,512]{1,0:T(1,128)S(1)} %copy-done.5), custom_call_target="tpu_custom_call" | custom-call | flops 2000000000 | bytes 3145728 | tf_op jit(solution)/shard_map/pallas_call | solution.py:203
  26.4 0.6 %collective-permute-start.3 = (bf16[1024,128]{1,0:T(8,128)(2,1)S(1)}, bf16[1024,128]{1,0:T(8,128)(2,1)S(1)}, u32[]{:S(2)}, u32[]{:S(2)}) collective-permute-start(bf16[1024,128]{1,0:T(8,128)(2,1)S(1)} %get-tuple-element.8.b0), channel_id=1, source_target_pairs={{3,0},{0,1},{1,2},{2,3},{7,4},{4,5},{5,6},{6,7},{11,8},{8,9},{9,10... | collective-permute-start | bytes 786440 | tf_op jit(solution)/shard_map/ppermute | solution.py:220
  26.9 1.5 %collective-permute-start = (bf16[1024,128]{1,0:T(8,128)(2,1)S(1)}, bf16[1024,128]{1,0:T(8,128)(2,1)S(1)}, u32[]{:S(2)}, u32[]{:S(2)}) collective-permute-start(bf16[1024,128]{1,0:T(8,128)(2,1)S(1)} %get-tuple-element.8.b0), channel_id=1, source_target_pairs={{1,0},{2,1},{3,2},{0,3},{5,4},{6,5},{7,6},{4,7},{9,8},{10,9},{11,1... | collective-permute-start | bytes 786440 | tf_op jit(solution)/shard_map/ppermute | solution.py:220
  28.5 1.4 %collective-permute-start.1 = (bf16[512,128]{1,0:T(8,128)(2,1)S(1)}, bf16[512,128]{1,0:T(8,128)(2,1)S(1)}, u32[]{:S(2)}, u32[]{:S(2)}) collective-permute-start(bf16[512,128]{1,0:T(8,128)(2,1)S(1)} %get-tuple-element.9), channel_id=1, source_target_pairs={{2,0},{3,1},{0,2},{1,3},{6,4},{7,5},{4,6},{5,7},{10,8},{11,9},{8,1... | collective-permute-start | bytes 393224 | tf_op jit(solution)/shard_map/ppermute | solution.py:220
  30.6 0.1 collective-permute-start.4
  30.7 2.2 %collective-permute-start.2 = (bf16[512,128]{1,0:T(8,128)(2,1)S(1)}, bf16[512,128]{1,0:T(8,128)(2,1)S(1)}, u32[]{:S(2)}, u32[]{:S(2)}) collective-permute-start(bf16[512,128]{1,0:T(8,128)(2,1)S(1)} %get-tuple-element.10), channel_id=1, source_target_pairs={{2,0},{3,1},{0,2},{1,3},{6,4},{7,5},{4,6},{5,7},{10,8},{11,9},{8,1... | collective-permute-start | bytes 393224 | tf_op jit(solution)/shard_map/ppermute | solution.py:220
  32.9 7.1 %collective-permute-done.1.g2 = bf16[512,128]{1,0:T(8,128)(2,1)S(1)} collective-permute-done((bf16[512,128]{1,0:T(8,128)(2,1)S(1)}, bf16[512,128]{1,0:T(8,128)(2,1)S(1)}, u32[]{:S(2)}, u32[]{:S(2)}) %collective-permute-start.1) | collective-permute-done | bytes 131104 | tf_op jit(solution)/shard_map/ppermute | solution.py:220
  40.0 0.0 collective-permute-done.3.b3
  40.0 0.6 %collective-permute-start.7 = (bf16[512,128]{1,0:T(8,128)(2,1)S(1)}, bf16[512,128]{1,0:T(8,128)(2,1)S(1)}, u32[]{:S(2)}, u32[]{:S(2)}) collective-permute-start(bf16[512,128]{1,0:T(8,128)(2,1)S(1)} %slice.9), channel_id=1, source_target_pairs={{0,4},{4,0},{8,12},{12,8},{16,20},{20,16},{24,28},{28,24},{32,36},... | collective-permute-start | bytes 393224 | tf_op jit(solution)/shard_map/ppermute | solution.py:223
  40.6 1.2 %collective-permute-done.b1 = bf16[1024,128]{1,0:T(8,128)(2,1)S(1)} collective-permute-done((bf16[1024,128]{1,0:T(8,128)(2,1)S(1)}, bf16[1024,128]{1,0:T(8,128)(2,1)S(1)}, u32[]{:S(2)}, u32[]{:S(2)}) %collective-permute-start) | collective-permute-done | bytes 262176 | tf_op jit(solution)/shard_map/ppermute | solution.py:220
  41.8 0.1 collective-permute-start.5
  41.9 0.1 fusion.10.index_ref
  42.0 0.0 collective-permute-done.2.o2
  42.0 0.0 collective-permute-done.4.s0
  42.0 0.0 collective-permute-done.6.s2
  42.0 0.0 collective-permute-done.7.s3
  42.0 1.2 %collective-permute-done.5.s1 = bf16[512,128]{1,0:T(8,128)(2,1)S(1)} collective-permute-done((bf16[512,128]{1,0:T(8,128)(2,1)S(1)}, bf16[512,128]{1,0:T(8,128)(2,1)S(1)}, u32[]{:S(2)}, u32[]{:S(2)}) %collective-permute-start.5) | collective-permute-done | bytes 131104 | tf_op jit(solution)/shard_map/ppermute | solution.py:223
  43.2 5.7 %shard_map.84 = f32[1024,1024]{1,0:T(8,128)} custom-call(s32[2048]{0:T(1024)S(1)} %fusion.10.index_ref, bf16[512,512]{1,0:T(8,128)(2,1)S(1)} %copy-done.3, bf16[512,512]{1,0:T(8,128)(2,1)S(1)} %copy-done.2, bf16[1024,128]{1,0:T(8,128)(2,1)S(1)} %get-tuple-element.8.b0, bf16[1024,128]{1,0:T(8,128)(2,1)S(1)} %collective-permute-done.b1, ...), custom_call_target="tpu_custom_call" | custom-call | flops 6000000000 | bytes 6291456 | tf_op jit(solution)/shard_map/pallas_call | solution.py:239
  (14 shorter events, 0.0 us)
Async XLA Ops:
  0.0 0.9 %copy-start = (bf16[1024,64]{0,1:T(8,128)(2,1)S(1)}, bf16[1024,64]{0,1:T(8,128)(2,1)}, u32[]{:S(2)}) copy-start(bf16[1024,64]{0,1:T(8,128)(2,1)} %param.8) | copy-start | bytes 393220
  0.9 24.4 %copy-start.1 = (bf16[1024,1024]{1,0:T(8,128)(2,1)S(1)}, bf16[1024,1024]{1,0:T(8,128)(2,1)}, u32[]{:S(2)}) copy-start(bf16[1024,1024]{1,0:T(8,128)(2,1)} %constant.99.clone.forward_ref) | copy-start | bytes 6291460
  0.9 24.4 %copy-start.4 = (bf16[512,512]{1,0:T(8,128)(2,1)S(1)}, bf16[512,512]{1,0:T(8,128)(2,1)}, u32[]{:S(2)}) copy-start(bf16[512,512]{1,0:T(8,128)(2,1)} %constant.100.clone.band_ref) | copy-start | bytes 1572868
  0.9 24.4 %copy-start.5 = (f32[1,512]{1,0:T(1,128)S(1)}, f32[1,512]{1,0:T(1,128)}, u32[]{:S(2)}) copy-start(f32[1,512]{1,0:T(1,128)} %constant.101.clone.share_ref) | copy-start | bytes 6148
  1.1 40.8 %copy-start.6 = (s32[8,128,2]{1,2,0:T(2,128)S(1)}, s32[8,128,2]{1,2,0:T(2,128)}, u32[]{:S(2)}) copy-start(s32[8,128,2]{1,2,0:T(2,128)} %param.9) | copy-start | bytes 24580
  1.1 42.1 %copy-start.2 = (bf16[512,512]{1,0:T(8,128)(2,1)S(1)}, bf16[512,512]{1,0:T(8,128)(2,1)}, u32[]{:S(2)}) copy-start(bf16[512,512]{1,0:T(8,128)(2,1)} %constant.103.clone.odd_ref) | copy-start | bytes 1572868
  1.1 42.1 %copy-start.3 = (bf16[512,512]{1,0:T(8,128)(2,1)S(1)}, bf16[512,512]{1,0:T(8,128)(2,1)}, u32[]{:S(2)}) copy-start(bf16[512,512]{1,0:T(8,128)(2,1)} %constant.102.clone.even_ref) | copy-start | bytes 1572868
  26.4 13.6 %collective-permute-start.3 = (bf16[1024,128]{1,0:T(8,128)(2,1)S(1)}, bf16[1024,128]{1,0:T(8,128)(2,1)S(1)}, u32[]{:S(2)}, u32[]{:S(2)}) collective-permute-start(bf16[1024,128]{1,0:T(8,128)(2,1)S(1)} %get-tuple-element.8.b0), channel_id=1, source_target_pairs={{3,0},{0,1},{1,2},{2,3},{7,4},{4,5},{5,6},{6,7},{11,8},{8,9},{9,10... | collective-permute-start | bytes 786440 | tf_op jit(solution)/shard_map/ppermute | solution.py:220
  26.9 14.8 %collective-permute-start = (bf16[1024,128]{1,0:T(8,128)(2,1)S(1)}, bf16[1024,128]{1,0:T(8,128)(2,1)S(1)}, u32[]{:S(2)}, u32[]{:S(2)}) collective-permute-start(bf16[1024,128]{1,0:T(8,128)(2,1)S(1)} %get-tuple-element.8.b0), channel_id=1, source_target_pairs={{1,0},{2,1},{3,2},{0,3},{5,4},{6,5},{7,6},{4,7},{9,8},{10,9},{11,1... | collective-permute-start | bytes 786440 | tf_op jit(solution)/shard_map/ppermute | solution.py:220
  28.5 11.5 %collective-permute-start.1 = (bf16[512,128]{1,0:T(8,128)(2,1)S(1)}, bf16[512,128]{1,0:T(8,128)(2,1)S(1)}, u32[]{:S(2)}, u32[]{:S(2)}) collective-permute-start(bf16[512,128]{1,0:T(8,128)(2,1)S(1)} %get-tuple-element.9), channel_id=1, source_target_pairs={{2,0},{3,1},{0,2},{1,3},{6,4},{7,5},{4,6},{5,7},{10,8},{11,9},{8,1... | collective-permute-start | bytes 393224 | tf_op jit(solution)/shard_map/ppermute | solution.py:220
  30.6 11.4 %collective-permute-start.4 = (bf16[512,128]{1,0:T(8,128)(2,1)S(1)}, bf16[512,128]{1,0:T(8,128)(2,1)S(1)}, u32[]{:S(2)}, u32[]{:S(2)}) collective-permute-start(bf16[512,128]{1,0:T(8,128)(2,1)S(1)} %get-tuple-element.9), channel_id=1, source_target_pairs={{0,4},{4,0},{8,12},{12,8},{16,20},{20,16},{24,28},{28,24},{32,36},... | collective-permute-start | bytes 393224 | tf_op jit(solution)/shard_map/ppermute | solution.py:223
  30.7 11.3 %collective-permute-start.2 = (bf16[512,128]{1,0:T(8,128)(2,1)S(1)}, bf16[512,128]{1,0:T(8,128)(2,1)S(1)}, u32[]{:S(2)}, u32[]{:S(2)}) collective-permute-start(bf16[512,128]{1,0:T(8,128)(2,1)S(1)} %get-tuple-element.10), channel_id=1, source_target_pairs={{2,0},{3,1},{0,2},{1,3},{6,4},{7,5},{4,6},{5,7},{10,8},{11,9},{8,1... | collective-permute-start | bytes 393224 | tf_op jit(solution)/shard_map/ppermute | solution.py:220
  40.0 2.0 %collective-permute-start.6 = (bf16[512,128]{1,0:T(8,128)(2,1)S(1)}, bf16[512,128]{1,0:T(8,128)(2,1)S(1)}, u32[]{:S(2)}, u32[]{:S(2)}) collective-permute-start(bf16[512,128]{1,0:T(8,128)(2,1)S(1)} %collective-permute-done.1.g2), channel_id=1, source_target_pairs={{0,4},{4,0},{8,12},{12,8},{16,20},{20,16},{24,28},{28,24},{32,36},... | collective-permute-start | bytes 393224 | tf_op jit(solution)/shard_map/ppermute | solution.py:223
  40.0 2.0 %collective-permute-start.7 = (bf16[512,128]{1,0:T(8,128)(2,1)S(1)}, bf16[512,128]{1,0:T(8,128)(2,1)S(1)}, u32[]{:S(2)}, u32[]{:S(2)}) collective-permute-start(bf16[512,128]{1,0:T(8,128)(2,1)S(1)} %slice.9), channel_id=1, source_target_pairs={{0,4},{4,0},{8,12},{12,8},{16,20},{20,16},{24,28},{28,24},{32,36},... | collective-permute-start | bytes 393224 | tf_op jit(solution)/shard_map/ppermute | solution.py:223
  41.8 1.4 %collective-permute-start.5 = (bf16[512,128]{1,0:T(8,128)(2,1)S(1)}, bf16[512,128]{1,0:T(8,128)(2,1)S(1)}, u32[]{:S(2)}, u32[]{:S(2)}) collective-permute-start(bf16[512,128]{1,0:T(8,128)(2,1)S(1)} %slice.8), channel_id=1, source_target_pairs={{0,4},{4,0},{8,12},{12,8},{16,20},{20,16},{24,28},{28,24},{32,36},... | collective-permute-start | bytes 393224 | tf_op jit(solution)/shard_map/ppermute | solution.py:223

commit v4 on v3

--- a/solution.py
+++ b/solution.py
@@ -60,7 +60,7 @@
 
 
 def whiten_kernel(
-    parts_ref, forward_ref, band_ref, share_ref, both_ref, given_ref, other_ref, segs, wide
+    parts_ref, forward_ref, band_ref, share_ref, given_ref, other_ref, segs, wide
 ):
     core = lax.rem(lax.axis_index("sta"), 2)
     low = lax.broadcasted_iota(jnp.int32, (PER, LANES), 1) < LANES // 2
@@ -103,34 +103,20 @@
                         wide[pl.ds(row, 8, stride=ROWS), :] = piece
     size = PER * ROWS
     given = 1 - core
-    given_rows = wide[pl.ds(pl.multiple_of(given * size, size), size), :].astype(jnp.bfloat16)
-    other_rows = wide[pl.ds(pl.multiple_of(core * size, size), size), :].astype(jnp.bfloat16)
-    both_ref[:size, :] = given_rows
-    both_ref[size:, :] = other_rows
-    given_ref[...] = given_rows
-    other_ref[...] = other_rows
-
-
-def pair_kernel(
-    index_ref, even_ref, odd_ref, b0, b1, g2, o2, b3, s0, s1, s2, s3, out_ref, *scratch
-):
+    given_ref[...] = wide[pl.ds(pl.multiple_of(given * size, size), size), :].astype(jnp.bfloat16)
+    other_ref[...] = wide[pl.ds(pl.multiple_of(core * size, size), size), :].astype(jnp.bfloat16)
+
+
+def pair_kernel(index_ref, even_ref, odd_ref, *refs):
+    sources, (out_ref, *scratch) = refs[: SLOTS * NETS], refs[SLOTS * NETS :]
     table, reals, imags, result, places, place_sem, sems = scratch
     size = PER * ROWS
     half = ROWS // 4
     pairs = index_ref.shape[0] // 2
     load_places = pltpu.make_async_copy(index_ref, places, place_sem)
     load_places.start()
-    sources = (
-        ((b0, 0), (b0, size), (s0, 0)),
-        ((b1, 0), (b1, size), (s1, 0)),
-        ((g2, 0), (o2, 0), (s2, 0)),
-        ((b3, 0), (b3, size), (s3, 0)),
-    )
-    for net in range(NETS):
-        for slot in range(SLOTS):
-            source, start = sources[net][slot]
-            row = (slot * NETS + net) * size
-            table[row : row + size, :] = source[start : start + size, :].astype(jnp.float32)
+    for n, source in enumerate(sources):
+        table[n * size : (n + 1) * size, :] = source[...].astype(jnp.float32)
     table[ZERO_ROW : ZERO_ROW + ROWS, :] = jnp.zeros((ROWS, LANES), jnp.float32)
     load_places.wait()
 
@@ -200,15 +186,14 @@
     ).reshape(columns * PER, LANES)
     band, share = band_tables()
     size = PER * ROWS
-    both, given, other = pl.pallas_call(
+    given, other = pl.pallas_call(
         whiten_kernel,
         out_shape=(
-            jax.ShapeDtypeStruct((2 * size, LANES), jnp.bfloat16),
             jax.ShapeDtypeStruct((size, LANES), jnp.bfloat16),
             jax.ShapeDtypeStruct((size, LANES), jnp.bfloat16),
         ),
         in_specs=[vmem] * 4,
-        out_specs=(vmem, vmem, vmem),
+        out_specs=(vmem, vmem),
         scratch_shapes=[
             pltpu.VMEM((2 * SEGMENTS * PER, POINTS), jnp.bfloat16),
             pltpu.VMEM((2 * size, LANES), jnp.float32),
@@ -222,10 +207,12 @@
     def from_other_core(value):
         return lax.ppermute(value, "sta", [(i, i ^ 1) for i in range(columns)])
 
-    other2, given2 = from_net(other, 2), from_net(given, 2)
-    both1, both3 = from_net(both, 1), from_net(both, 3)
-    pieces = [both, both1, given2, other2, both3]
-    swapped = [from_other_core(part) for part in (given, both1[:size], given2, both3[:size])]
+    other3, given1 = from_net(other, 3), from_net(given, 1)
+    other1, given3 = from_net(other, 1), from_net(given, 3)
+    other2, given2 = from_net(other1, 1), from_net(given3, 3)
+    first, third, other1 = lax.optimization_barrier((given, given3, other1))
+    givens = [given, given1, given2, given3]
+    pieces = givens + [other, other1, other2, other3] + [from_other_core(part) for part in (first, given1, given2, third)]
 
     station_net = pair_list // (columns * PER)
     offset = pair_list // PER % columns - column
@@ -239,7 +226,7 @@
     return pl.pallas_call(
         pair_kernel,
         out_shape=jax.ShapeDtypeStruct((pairs, POINTS), jnp.float32),
-        in_specs=[vmem] * 12,
+        in_specs=[vmem] * (3 + SLOTS * NETS),
         out_specs=pl.BlockSpec(memory_space=pl.ANY),
         scratch_shapes=[
             pltpu.VMEM((ZERO_ROW + ROWS, LANES), jnp.float32),
@@ -252,7 +239,7 @@
         ],
         compiler_params=pltpu.CompilerParams(vmem_limit_bytes=24 * 2**20),
         cost_estimate=pl.CostEstimate(flops=6 * 10**9, bytes_accessed=6 * 2**20, transcendentals=0),
-    )(index, jnp.asarray(even), jnp.asarray(odd), *pieces, *swapped).reshape(
+    )(index, jnp.asarray(even), jnp.asarray(odd), *pieces).reshape(
         pair_list.shape[0], BLOCK, POINTS
     )
 

time: 49.6 us -> 47.6 us (0.960); the launches traced: 48.9 us -> 47.5 us
  waiting for transfers between devices: 9.51 us -> 8.26 us
    ppermute x4, waiting for transfers between devices: 1.23 us -> 0.01 us  [from_other_core(): return lax.ppermute(value, 'sta', [(i, i ^ 1) for i in range(columns)])]
    ppermute x4 -> x6, starting transfers between devices: 5.72 us -> 5.82 us  [from_net(): lax.ppermute(value, 'grp', [((i + by) % nets, i) for i in range(nets)])]
    ppermute x4 -> x6, waiting for transfers between devices: 8.28 us -> 8.25 us  [from_net(): lax.ppermute(value, 'grp', [((i + by) % nets, i) for i in range(nets)])]
  transfers between devices with their start and end apart: 8 -> 10, of which waited for: 3 -> 4; matrix products, arithmetic and copies ran while one was open for 0% -> 0% of each run, Pallas kernels for 0% -> 0%
where the time goes in v4:
time: 47.6 us; the launch traced here: 47.5 us
  blocking collectives  24.2 us (51%)
  waiting for transfers between devices  8.26 us (17%)
  Pallas kernels  6.9 us (14%)
  starting transfers between devices  6.41 us (13%)
  local copies, waits for them, and re-layouts  0.93 us (2%)
  between operations  0.76 us (2%)
    all_to_all x1, blocking collectives, local(): lax.all_to_all(messages.reshape(columns, PER, LANES), 'sta', split_axis=0...  24.2 us
    ppermute x6, waiting for transfers between devices, from_net(): lax.ppermute(value, 'grp', [((i + by) % nets, i) for i in range(nets)])  8.25 us
    ppermute x6, starting transfers between devices, from_net(): lax.ppermute(value, 'grp', [((i + by) % nets, i) for i in range(nets)])  5.82 us
    pallas_call x1, Pallas kernels, local(): pl.pallas_call(pair_kernel, out_shape=jax.ShapeDtypeStruct((pairs, POINTS...  5.67 us
    pallas_call x1, Pallas kernels, local(): pl.pallas_call(whiten_kernel, out_shape=(jax.ShapeDtypeStruct((size, LANE...  1.03 us
  transfers between devices with their start and end apart: 10, of which 4 were waited for; matrix products, arithmetic and copies ran while one was open for 0% of the time, Pallas kernels for 0%

profile of v4, /device:TPU:6, one launch (start us, length us, event | category | flops | bytes accessed | tf_op | source)
XLA Modules:
  0.0 47.5 jit_solution(13686043763034382059)
XLA Ops:
  0.0 0.9 %copy-done = bf16[1024,64]{0,1:T(8,128)(2,1)S(1)} copy-done((bf16[1024,64]{0,1:T(8,128)(2,1)S(1)}, bf16[1024,64]{0,1:T(8,128)(2,1)}, u32[]{:S(2)}) %copy-start) | copy-done | bytes 131096
  0.9 0.2 shard_map.82
  1.1 0.0 copy-start.6
  1.1 0.0 copy-start.2
  1.1 0.0 copy-start.3
  1.2 24.2 %all_to_all.5 = bf16[64,16,128]{2,1,0:T(8,128)(2,1)S(1)} all-to-all(bf16[64,16,128]{2,1,0:T(8,128)(2,1)S(1)} %bitcast.11), channel_id=1, replica_groups=mesh['sta'=64,'grp'=4] {'sta'}, dimensions={0} | all-to-all | bytes 524288 | tf_op jit(solution)/shard_map/all_to_all | solution.py:184
  25.3 1.0 %shard_map.83 = (bf16[512,128]{1,0:T(8,128)(2,1)S(1)}, bf16[512,128]{1,0:T(8,128)(2,1)S(1)}) custom-call(bf16[1024,128]{1,0:T(8,128)(2,1)S(1)} %bitcast.10, bf16[1024,1024]{1,0:T(8,128)(2,1)S(1)} %copy-done.1, bf16[512,512]{1,0:T(8,128)(2,1)S(1)} %copy-done.4, f32[1,512]{1,0:T(1,128)S(1)} %copy-done.5), custom_call_target="tpu_custom_call" | custom-call | flops 2000000000 | bytes 3145728 | tf_op jit(solution)/shard_map/pallas_call | solution.py:189
  26.4 0.6 %collective-permute-start.1 = (bf16[512,128]{1,0:T(8,128)(2,1)S(1)}, bf16[512,128]{1,0:T(8,128)(2,1)S(1)}, u32[]{:S(2)}, u32[]{:S(2)}) collective-permute-start(bf16[512,128]{1,0:T(8,128)(2,1)S(1)} %get-tuple-element.13.refs_0_), channel_id=1, source_target_pairs={{3,0},{0,1},{1,2},{2,3},{7,4},{4,5},{5,6},{6,7},{11,8},{8,9},{9,10... | collective-permute-start | bytes 393224 | tf_op jit(solution)/shard_map/ppermute | solution.py:205
  26.9 1.5 %collective-permute-start.3 = (bf16[512,128]{1,0:T(8,128)(2,1)S(1)}, bf16[512,128]{1,0:T(8,128)(2,1)S(1)}, u32[]{:S(2)}, u32[]{:S(2)}) collective-permute-start(bf16[512,128]{1,0:T(8,128)(2,1)S(1)} %get-tuple-element.11.refs_4_), channel_id=1, source_target_pairs={{1,0},{2,1},{3,2},{0,3},{5,4},{6,5},{7,6},{4,7},{9,8},{10,9},{11,1... | collective-permute-start | bytes 393224 | tf_op jit(solution)/shard_map/ppermute | solution.py:205
  28.5 1.7 %collective-permute-start.5 = (bf16[512,128]{1,0:T(8,128)(2,1)S(1)}, bf16[512,128]{1,0:T(8,128)(2,1)S(1)}, u32[]{:S(2)}, u32[]{:S(2)}) collective-permute-start(bf16[512,128]{1,0:T(8,128)(2,1)S(1)} %get-tuple-element.11.refs_4_), channel_id=1, source_target_pairs={{3,0},{0,1},{1,2},{2,3},{7,4},{4,5},{5,6},{6,7},{11,8},{8,9},{9,10... | collective-permute-start | bytes 393224 | tf_op jit(solution)/shard_map/ppermute | solution.py:205
  30.2 0.3 collective-permute-start
  30.5 2.3 %collective-permute-done.1.refs_3_ = bf16[512,128]{1,0:T(8,128)(2,1)S(1)} collective-permute-done((bf16[512,128]{1,0:T(8,128)(2,1)S(1)}, bf16[512,128]{1,0:T(8,128)(2,1)S(1)}, u32[]{:S(2)}, u32[]{:S(2)}) %collective-permute-start.1) | collective-permute-done | bytes 131104 | tf_op jit(solution)/shard_map/ppermute | solution.py:205
  32.8 0.9 %collective-permute-start.2 = (bf16[512,128]{1,0:T(8,128)(2,1)S(1)}, bf16[512,128]{1,0:T(8,128)(2,1)S(1)}, u32[]{:S(2)}, u32[]{:S(2)}) collective-permute-start(bf16[512,128]{1,0:T(8,128)(2,1)S(1)} %collective-permute-done.1.refs_3_), channel_id=1, source_target_pairs={{3,0},{0,1},{1,2},{2,3},{7,4},{4,5},{5,6},{6,7},{11,8},{8,9},{9,10... | collective-permute-start | bytes 393224 | tf_op jit(solution)/shard_map/ppermute | solution.py:205
  34.3 0.0 collective-permute-done.3.refs_5_
  34.3 0.1 collective-permute-start.6
  34.4 0.5 %collective-permute-start.9 = (bf16[512,128]{1,0:T(8,128)(2,1)S(1)}, bf16[512,128]{1,0:T(8,128)(2,1)S(1)}, u32[]{:S(2)}, u32[]{:S(2)}) collective-permute-start(bf16[512,128]{1,0:T(8,128)(2,1)S(1)} %collective-permute-done.1.refs_3_), channel_id=1, source_target_pairs={{0,4},{4,0},{8,12},{12,8},{16,20},{20,16},{24,28},{28,24},{32,36},... | collective-permute-start | bytes 393224 | tf_op jit(solution)/shard_map/ppermute | solution.py:208
  34.9 0.7 %collective-permute-done.5.refs_7_ = bf16[512,128]{1,0:T(8,128)(2,1)S(1)} collective-permute-done((bf16[512,128]{1,0:T(8,128)(2,1)S(1)}, bf16[512,128]{1,0:T(8,128)(2,1)S(1)}, u32[]{:S(2)}, u32[]{:S(2)}) %collective-permute-start.5) | collective-permute-done | bytes 131104 | tf_op jit(solution)/shard_map/ppermute | solution.py:205
  35.6 0.8 %collective-permute-start.4 = (bf16[512,128]{1,0:T(8,128)(2,1)S(1)}, bf16[512,128]{1,0:T(8,128)(2,1)S(1)}, u32[]{:S(2)}, u32[]{:S(2)}) collective-permute-start(bf16[512,128]{1,0:T(8,128)(2,1)S(1)} %collective-permute-done.3.refs_5_), channel_id=1, source_target_pairs={{1,0},{2,1},{3,2},{0,3},{5,4},{6,5},{7,6},{4,7},{9,8},{10,9},{11,1... | collective-permute-start | bytes 393224 | tf_op jit(solution)/shard_map/ppermute | solution.py:205
  36.4 0.0 collective-permute-done.refs_1_
  36.4 0.0 collective-permute-start.7
  36.4 1.3 %collective-permute-done.2.refs_2_ = bf16[512,128]{1,0:T(8,128)(2,1)S(1)} collective-permute-done((bf16[512,128]{1,0:T(8,128)(2,1)S(1)}, bf16[512,128]{1,0:T(8,128)(2,1)S(1)}, u32[]{:S(2)}, u32[]{:S(2)}) %collective-permute-start.2) | collective-permute-done | bytes 131104 | tf_op jit(solution)/shard_map/ppermute | solution.py:205
  37.8 0.1 fusion.10.index_ref
  37.8 3.9 %collective-permute-done.4.refs_6_ = bf16[512,128]{1,0:T(8,128)(2,1)S(1)} collective-permute-done((bf16[512,128]{1,0:T(8,128)(2,1)S(1)}, bf16[512,128]{1,0:T(8,128)(2,1)S(1)}, u32[]{:S(2)}, u32[]{:S(2)}) %collective-permute-start.4) | collective-permute-done | bytes 131104 | tf_op jit(solution)/shard_map/ppermute | solution.py:205
  41.8 5.7 %shard_map.84 = f32[1024,1024]{1,0:T(8,128)} custom-call(s32[2048]{0:T(1024)S(1)} %fusion.10.index_ref, bf16[512,512]{1,0:T(8,128)(2,1)S(1)} %copy-done.3, bf16[512,512]{1,0:T(8,128)(2,1)S(1)} %copy-done.2, bf16[512,128]{1,0:T(8,128)(2,1)S(1)} %get-tuple-element.13.refs_0_, bf16[512,128]{1,0:T(8,128)(2,1)S(1)} %collective-permute-done.refs_1_, ...), custom_call_target="tpu_custom_call" | custom-call | flops 6000000000 | bytes 6291456 | tf_op jit(solution)/shard_map/pallas_call | solution.py:226
  (16 shorter events, 0.0 us)
Async XLA Ops:
  0.0 0.9 %copy-start = (bf16[1024,64]{0,1:T(8,128)(2,1)S(1)}, bf16[1024,64]{0,1:T(8,128)(2,1)}, u32[]{:S(2)}) copy-start(bf16[1024,64]{0,1:T(8,128)(2,1)} %param.8) | copy-start | bytes 393220
  0.9 24.4 %copy-start.1 = (bf16[1024,1024]{1,0:T(8,128)(2,1)S(1)}, bf16[1024,1024]{1,0:T(8,128)(2,1)}, u32[]{:S(2)}) copy-start(bf16[1024,1024]{1,0:T(8,128)(2,1)} %constant.99.clone.forward_ref) | copy-start | bytes 6291460
  0.9 24.4 %copy-start.4 = (bf16[512,512]{1,0:T(8,128)(2,1)S(1)}, bf16[512,512]{1,0:T(8,128)(2,1)}, u32[]{:S(2)}) copy-start(bf16[512,512]{1,0:T(8,128)(2,1)} %constant.100.clone.band_ref) | copy-start | bytes 1572868
  0.9 24.4 %copy-start.5 = (f32[1,512]{1,0:T(1,128)S(1)}, f32[1,512]{1,0:T(1,128)}, u32[]{:S(2)}) copy-start(f32[1,512]{1,0:T(1,128)} %constant.101.clone.share_ref) | copy-start | bytes 6148
  1.1 36.6 %copy-start.6 = (s32[8,128,2]{1,2,0:T(2,128)S(1)}, s32[8,128,2]{1,2,0:T(2,128)}, u32[]{:S(2)}) copy-start(s32[8,128,2]{1,2,0:T(2,128)} %param.9) | copy-start | bytes 24580
  1.1 40.7 %copy-start.2 = (bf16[512,512]{1,0:T(8,128)(2,1)S(1)}, bf16[512,512]{1,0:T(8,128)(2,1)}, u32[]{:S(2)}) copy-start(bf16[512,512]{1,0:T(8,128)(2,1)} %constant.103.clone.odd_ref) | copy-start | bytes 1572868
  1.1 40.7 %copy-start.3 = (bf16[512,512]{1,0:T(8,128)(2,1)S(1)}, bf16[512,512]{1,0:T(8,128)(2,1)}, u32[]{:S(2)}) copy-start(bf16[512,512]{1,0:T(8,128)(2,1)} %constant.102.clone.even_ref) | copy-start | bytes 1572868
  26.4 6.4 %collective-permute-start.1 = (bf16[512,128]{1,0:T(8,128)(2,1)S(1)}, bf16[512,128]{1,0:T(8,128)(2,1)S(1)}, u32[]{:S(2)}, u32[]{:S(2)}) collective-permute-start(bf16[512,128]{1,0:T(8,128)(2,1)S(1)} %get-tuple-element.13.refs_0_), channel_id=1, source_target_pairs={{3,0},{0,1},{1,2},{2,3},{7,4},{4,5},{5,6},{6,7},{11,8},{8,9},{9,10... | collective-permute-start | bytes 393224 | tf_op jit(solution)/shard_map/ppermute | solution.py:205
  26.9 7.4 %collective-permute-start.3 = (bf16[512,128]{1,0:T(8,128)(2,1)S(1)}, bf16[512,128]{1,0:T(8,128)(2,1)S(1)}, u32[]{:S(2)}, u32[]{:S(2)}) collective-permute-start(bf16[512,128]{1,0:T(8,128)(2,1)S(1)} %get-tuple-element.11.refs_4_), channel_id=1, source_target_pairs={{1,0},{2,1},{3,2},{0,3},{5,4},{6,5},{7,6},{4,7},{9,8},{10,9},{11,1... | collective-permute-start | bytes 393224 | tf_op jit(solution)/shard_map/ppermute | solution.py:205
  28.5 7.1 %collective-permute-start.5 = (bf16[512,128]{1,0:T(8,128)(2,1)S(1)}, bf16[512,128]{1,0:T(8,128)(2,1)S(1)}, u32[]{:S(2)}, u32[]{:S(2)}) collective-permute-start(bf16[512,128]{1,0:T(8,128)(2,1)S(1)} %get-tuple-element.11.refs_4_), channel_id=1, source_target_pairs={{3,0},{0,1},{1,2},{2,3},{7,4},{4,5},{5,6},{6,7},{11,8},{8,9},{9,10... | collective-permute-start | bytes 393224 | tf_op jit(solution)/shard_map/ppermute | solution.py:205
  30.2 6.3 %collective-permute-start = (bf16[512,128]{1,0:T(8,128)(2,1)S(1)}, bf16[512,128]{1,0:T(8,128)(2,1)S(1)}, u32[]{:S(2)}, u32[]{:S(2)}) collective-permute-start(bf16[512,128]{1,0:T(8,128)(2,1)S(1)} %get-tuple-element.13.refs_0_), channel_id=1, source_target_pairs={{1,0},{2,1},{3,2},{0,3},{5,4},{6,5},{7,6},{4,7},{9,8},{10,9},{11,1... | collective-permute-start | bytes 393224 | tf_op jit(solution)/shard_map/ppermute | solution.py:205
  32.8 5.0 %collective-permute-start.2 = (bf16[512,128]{1,0:T(8,128)(2,1)S(1)}, bf16[512,128]{1,0:T(8,128)(2,1)S(1)}, u32[]{:S(2)}, u32[]{:S(2)}) collective-permute-start(bf16[512,128]{1,0:T(8,128)(2,1)S(1)} %collective-permute-done.1.refs_3_), channel_id=1, source_target_pairs={{3,0},{0,1},{1,2},{2,3},{7,4},{4,5},{5,6},{6,7},{11,8},{8,9},{9,10... | collective-permute-start | bytes 393224 | tf_op jit(solution)/shard_map/ppermute | solution.py:205
  34.3 7.5 %collective-permute-start.6 = (bf16[512,128]{1,0:T(8,128)(2,1)S(1)}, bf16[512,128]{1,0:T(8,128)(2,1)S(1)}, u32[]{:S(2)}, u32[]{:S(2)}) collective-permute-start(bf16[512,128]{1,0:T(8,128)(2,1)S(1)} %get-tuple-element.13.refs_0_), channel_id=1, source_target_pairs={{0,4},{4,0},{8,12},{12,8},{16,20},{20,16},{24,28},{28,24},{32,36},... | collective-permute-start | bytes 393224 | tf_op jit(solution)/shard_map/ppermute | solution.py:208
  34.4 7.4 %collective-permute-start.9 = (bf16[512,128]{1,0:T(8,128)(2,1)S(1)}, bf16[512,128]{1,0:T(8,128)(2,1)S(1)}, u32[]{:S(2)}, u32[]{:S(2)}) collective-permute-start(bf16[512,128]{1,0:T(8,128)(2,1)S(1)} %collective-permute-done.1.refs_3_), channel_id=1, source_target_pairs={{0,4},{4,0},{8,12},{12,8},{16,20},{20,16},{24,28},{28,24},{32,36},... | collective-permute-start | bytes 393224 | tf_op jit(solution)/shard_map/ppermute | solution.py:208
  35.6 6.2 %collective-permute-start.4 = (bf16[512,128]{1,0:T(8,128)(2,1)S(1)}, bf16[512,128]{1,0:T(8,128)(2,1)S(1)}, u32[]{:S(2)}, u32[]{:S(2)}) collective-permute-start(bf16[512,128]{1,0:T(8,128)(2,1)S(1)} %collective-permute-done.3.refs_5_), channel_id=1, source_target_pairs={{1,0},{2,1},{3,2},{0,3},{5,4},{6,5},{7,6},{4,7},{9,8},{10,9},{11,1... | collective-permute-start | bytes 393224 | tf_op jit(solution)/shard_map/ppermute | solution.py:205
  36.4 5.4 %collective-permute-start.7 = (bf16[512,128]{1,0:T(8,128)(2,1)S(1)}, bf16[512,128]{1,0:T(8,128)(2,1)S(1)}, u32[]{:S(2)}, u32[]{:S(2)}) collective-permute-start(bf16[512,128]{1,0:T(8,128)(2,1)S(1)} %collective-permute-done.refs_1_), channel_id=1, source_target_pairs={{0,4},{4,0},{8,12},{12,8},{16,20},{20,16},{24,28},{28,24},{32,36},... | collective-permute-start | bytes 393224 | tf_op jit(solution)/shard_map/ppermute | solution.py:208
  37.8 4.0 %collective-permute-start.8 = (bf16[512,128]{1,0:T(8,128)(2,1)S(1)}, bf16[512,128]{1,0:T(8,128)(2,1)S(1)}, u32[]{:S(2)}, u32[]{:S(2)}) collective-permute-start(bf16[512,128]{1,0:T(8,128)(2,1)S(1)} %collective-permute-done.2.refs_2_), channel_id=1, source_target_pairs={{0,4},{4,0},{8,12},{12,8},{16,20},{20,16},{24,28},{28,24},{32,36},... | collective-permute-start | bytes 393224 | tf_op jit(solution)/shard_map/ppermute | solution.py:208

commit v5 on v4

--- a/solution.py
+++ b/solution.py
@@ -107,7 +107,7 @@
     other_ref[...] = wide[pl.ds(pl.multiple_of(core * size, size), size), :].astype(jnp.bfloat16)
 
 
-def pair_kernel(index_ref, even_ref, odd_ref, *refs):
+def pair_kernel(live_ref, index_ref, even_ref, odd_ref, *refs):
     sources, (out_ref, *scratch) = refs[: SLOTS * NETS], refs[SLOTS * NETS :]
     table, reals, imags, result, places, place_sem, sems = scratch
     size = PER * ROWS
@@ -115,6 +115,22 @@
     pairs = index_ref.shape[0] // 2
     load_places = pltpu.make_async_copy(index_ref, places, place_sem)
     load_places.start()
+    steps = pairs // STEP_PAIRS
+    busy = jnp.minimum(lax.div(live_ref[0] * BLOCK + STEP_PAIRS - 1, STEP_PAIRS), steps)
+
+    def rows_at(step):
+        return pl.ds(pl.multiple_of(step * STEP_PAIRS, STEP_PAIRS), STEP_PAIRS)
+
+    def send(step):
+        rows = rows_at(step)
+        return pltpu.make_async_copy(result.at[rows], out_ref.at[rows], sems.at[step])
+
+    def clear(step, carry):
+        result[rows_at(step), :] = jnp.zeros((STEP_PAIRS, POINTS), jnp.float32)
+        send(step).start()
+        return carry
+
+    lax.fori_loop(busy, steps, clear, 0)
     for n, source in enumerate(sources):
         table[n * size : (n + 1) * size, :] = source[...].astype(jnp.float32)
     table[ZERO_ROW : ZERO_ROW + ROWS, :] = jnp.zeros((ROWS, LANES), jnp.float32)
@@ -139,10 +155,6 @@
                 blocks.append((low + high).astype(jnp.bfloat16))
         return jnp.concatenate(blocks, axis=1)
 
-    def send(step):
-        rows = pl.ds(pl.multiple_of(step * STEP_PAIRS, STEP_PAIRS), STEP_PAIRS)
-        return pltpu.make_async_copy(result.at[rows], out_ref.at[rows], sems.at[step])
-
     def run(step, carry):
         def some(g, inner):
             for q in range(UNROLL):
@@ -152,7 +164,7 @@
         lax.fori_loop(0, STEP_PAIRS // UNROLL, some, 0)
         even = jnp.dot(rows_of(0), even_ref[...], preferred_element_type=jnp.float32)
         odd = jnp.dot(rows_of(2), odd_ref[...], preferred_element_type=jnp.float32)
-        here = pl.ds(pl.multiple_of(step * STEP_PAIRS, STEP_PAIRS), STEP_PAIRS)
+        here = rows_at(step)
         result[here, : POINTS // 2] = even + odd
         result[here, POINTS // 2 :] = even - odd
         send(step).start()
@@ -162,8 +174,8 @@
         send(step).wait()
         return carry
 
-    lax.fori_loop(0, pairs // STEP_PAIRS, run, 0)
-    lax.fori_loop(0, pairs // STEP_PAIRS, finish, 0)
+    lax.fori_loop(0, busy, run, 0)
+    lax.fori_loop(0, steps, finish, 0)
 
 
 def local(records, pair_list, live_blocks):
@@ -226,7 +238,7 @@
     return pl.pallas_call(
         pair_kernel,
         out_shape=jax.ShapeDtypeStruct((pairs, POINTS), jnp.float32),
-        in_specs=[vmem] * (3 + SLOTS * NETS),
+        in_specs=[pl.BlockSpec(memory_space=pltpu.SMEM)] + [vmem] * (3 + SLOTS * NETS),
         out_specs=pl.BlockSpec(memory_space=pl.ANY),
         scratch_shapes=[
             pltpu.VMEM((ZERO_ROW + ROWS, LANES), jnp.float32),
@@ -239,7 +251,7 @@
         ],
         compiler_params=pltpu.CompilerParams(vmem_limit_bytes=24 * 2**20),
         cost_estimate=pl.CostEstimate(flops=6 * 10**9, bytes_accessed=6 * 2**20, transcendentals=0),
-    )(index, jnp.asarray(even), jnp.asarray(odd), *pieces).reshape(
+    )(live_blocks, index, jnp.asarray(even), jnp.asarray(odd), *pieces).reshape(
         pair_list.shape[0], BLOCK, POINTS
     )
 

time: 47.6 us -> 47.1 us (0.989); the launches traced: 47.5 us -> 47.5 us
  no operation moved by 1% of the time
where the time goes in v5:
time: 47.1 us; the launch traced here: 47.5 us
  blocking collectives  24.2 us (51%)
  waiting for transfers between devices  8.26 us (18%)
  Pallas kernels  6.9 us (15%)
  starting transfers between devices  6.41 us (14%)
  local copies, waits for them, and re-layouts  0.93 us (2%)
  between operations  0.76 us (2%)
    all_to_all x1, blocking collectives, local(): lax.all_to_all(messages.reshape(columns, PER, LANES), 'sta', split_axis=0...  24.2 us
    ppermute x6, waiting for transfers between devices, from_net(): lax.ppermute(value, 'grp', [((i + by) % nets, i) for i in range(nets)])  8.24 us
    ppermute x6, starting transfers between devices, from_net(): lax.ppermute(value, 'grp', [((i + by) % nets, i) for i in range(nets)])  5.82 us
    pallas_call x1, Pallas kernels, local(): pl.pallas_call(pair_kernel, out_shape=jax.ShapeDtypeStruct((pairs, POINTS...  5.67 us
    pallas_call x1, Pallas kernels, local(): pl.pallas_call(whiten_kernel, out_shape=(jax.ShapeDtypeStruct((size, LANE...  1.03 us
  transfers between devices with their start and end apart: 10, of which 4 were waited for; matrix products, arithmetic and copies ran while one was open for 0% of the time, Pallas kernels for 0%

profile of v5, /device:TPU:6, one launch (start us, length us, event | category | flops | bytes accessed | tf_op | source)
XLA Modules:
  0.0 47.5 jit_solution(14670109198054181998)
XLA Ops:
  0.0 0.9 %copy-done = bf16[1024,64]{0,1:T(8,128)(2,1)S(1)} copy-done((bf16[1024,64]{0,1:T(8,128)(2,1)S(1)}, bf16[1024,64]{0,1:T(8,128)(2,1)}, u32[]{:S(2)}) %copy-start) | copy-done | bytes 131096
  0.9 0.2 shard_map.82
  1.1 0.0 copy-start.6
  1.1 0.0 copy-start.2
  1.1 0.0 copy-start.3
  1.2 24.2 %all_to_all.5 = bf16[64,16,128]{2,1,0:T(8,128)(2,1)S(1)} all-to-all(bf16[64,16,128]{2,1,0:T(8,128)(2,1)S(1)} %bitcast.11), channel_id=1, replica_groups=mesh['sta'=64,'grp'=4] {'sta'}, dimensions={0} | all-to-all | bytes 524288 | tf_op jit(solution)/shard_map/all_to_all | solution.py:196
  25.3 1.0 %shard_map.83 = (bf16[512,128]{1,0:T(8,128)(2,1)S(1)}, bf16[512,128]{1,0:T(8,128)(2,1)S(1)}) custom-call(bf16[1024,128]{1,0:T(8,128)(2,1)S(1)} %bitcast.10, bf16[1024,1024]{1,0:T(8,128)(2,1)S(1)} %copy-done.1, bf16[512,512]{1,0:T(8,128)(2,1)S(1)} %copy-done.4, f32[1,512]{1,0:T(1,128)S(1)} %copy-done.5), custom_call_target="tpu_custom_call" | custom-call | flops 2000000000 | bytes 3145728 | tf_op jit(solution)/shard_map/pallas_call | solution.py:201
  26.4 0.6 %collective-permute-start.1 = (bf16[512,128]{1,0:T(8,128)(2,1)S(1)}, bf16[512,128]{1,0:T(8,128)(2,1)S(1)}, u32[]{:S(2)}, u32[]{:S(2)}) collective-permute-start(bf16[512,128]{1,0:T(8,128)(2,1)S(1)} %get-tuple-element.13.refs_0_), channel_id=1, source_target_pairs={{3,0},{0,1},{1,2},{2,3},{7,4},{4,5},{5,6},{6,7},{11,8},{8,9},{9,10... | collective-permute-start | bytes 393224 | tf_op jit(solution)/shard_map/ppermute | solution.py:217
  26.9 1.5 %collective-permute-start.3 = (bf16[512,128]{1,0:T(8,128)(2,1)S(1)}, bf16[512,128]{1,0:T(8,128)(2,1)S(1)}, u32[]{:S(2)}, u32[]{:S(2)}) collective-permute-start(bf16[512,128]{1,0:T(8,128)(2,1)S(1)} %get-tuple-element.11.refs_4_), channel_id=1, source_target_pairs={{1,0},{2,1},{3,2},{0,3},{5,4},{6,5},{7,6},{4,7},{9,8},{10,9},{11,1... | collective-permute-start | bytes 393224 | tf_op jit(solution)/shard_map/ppermute | solution.py:217
  28.5 1.7 %collective-permute-start.5 = (bf16[512,128]{1,0:T(8,128)(2,1)S(1)}, bf16[512,128]{1,0:T(8,128)(2,1)S(1)}, u32[]{:S(2)}, u32[]{:S(2)}) collective-permute-start(bf16[512,128]{1,0:T(8,128)(2,1)S(1)} %get-tuple-element.11.refs_4_), channel_id=1, source_target_pairs={{3,0},{0,1},{1,2},{2,3},{7,4},{4,5},{5,6},{6,7},{11,8},{8,9},{9,10... | collective-permute-start | bytes 393224 | tf_op jit(solution)/shard_map/ppermute | solution.py:217
  30.2 0.3 collective-permute-start
  30.5 2.3 %collective-permute-done.1.refs_3_ = bf16[512,128]{1,0:T(8,128)(2,1)S(1)} collective-permute-done((bf16[512,128]{1,0:T(8,128)(2,1)S(1)}, bf16[512,128]{1,0:T(8,128)(2,1)S(1)}, u32[]{:S(2)}, u32[]{:S(2)}) %collective-permute-start.1) | collective-permute-done | bytes 131104 | tf_op jit(solution)/shard_map/ppermute | solution.py:217
  32.8 0.9 %collective-permute-start.2 = (bf16[512,128]{1,0:T(8,128)(2,1)S(1)}, bf16[512,128]{1,0:T(8,128)(2,1)S(1)}, u32[]{:S(2)}, u32[]{:S(2)}) collective-permute-start(bf16[512,128]{1,0:T(8,128)(2,1)S(1)} %collective-permute-done.1.refs_3_), channel_id=1, source_target_pairs={{3,0},{0,1},{1,2},{2,3},{7,4},{4,5},{5,6},{6,7},{11,8},{8,9},{9,10... | collective-permute-start | bytes 393224 | tf_op jit(solution)/shard_map/ppermute | solution.py:217
  34.3 0.0 collective-permute-done.3.refs_5_
  34.3 0.1 collective-permute-start.6
  34.4 0.5 %collective-permute-start.9 = (bf16[512,128]{1,0:T(8,128)(2,1)S(1)}, bf16[512,128]{1,0:T(8,128)(2,1)S(1)}, u32[]{:S(2)}, u32[]{:S(2)}) collective-permute-start(bf16[512,128]{1,0:T(8,128)(2,1)S(1)} %collective-permute-done.1.refs_3_), channel_id=1, source_target_pairs={{0,4},{4,0},{8,12},{12,8},{16,20},{20,16},{24,28},{28,24},{32,36},... | collective-permute-start | bytes 393224 | tf_op jit(solution)/shard_map/ppermute | solution.py:220
  34.9 0.7 %collective-permute-done.5.refs_7_ = bf16[512,128]{1,0:T(8,128)(2,1)S(1)} collective-permute-done((bf16[512,128]{1,0:T(8,128)(2,1)S(1)}, bf16[512,128]{1,0:T(8,128)(2,1)S(1)}, u32[]{:S(2)}, u32[]{:S(2)}) %collective-permute-start.5) | collective-permute-done | bytes 131104 | tf_op jit(solution)/shard_map/ppermute | solution.py:217
  35.6 0.8 %collective-permute-start.4 = (bf16[512,128]{1,0:T(8,128)(2,1)S(1)}, bf16[512,128]{1,0:T(8,128)(2,1)S(1)}, u32[]{:S(2)}, u32[]{:S(2)}) collective-permute-start(bf16[512,128]{1,0:T(8,128)(2,1)S(1)} %collective-permute-done.3.refs_5_), channel_id=1, source_target_pairs={{1,0},{2,1},{3,2},{0,3},{5,4},{6,5},{7,6},{4,7},{9,8},{10,9},{11,1... | collective-permute-start | bytes 393224 | tf_op jit(solution)/shard_map/ppermute | solution.py:217
  36.4 0.0 collective-permute-start.7
  36.4 1.3 %collective-permute-done.2.refs_2_ = bf16[512,128]{1,0:T(8,128)(2,1)S(1)} collective-permute-done((bf16[512,128]{1,0:T(8,128)(2,1)S(1)}, bf16[512,128]{1,0:T(8,128)(2,1)S(1)}, u32[]{:S(2)}, u32[]{:S(2)}) %collective-permute-start.2) | collective-permute-done | bytes 131104 | tf_op jit(solution)/shard_map/ppermute | solution.py:217
  37.8 0.1 fusion.10.index_ref
  37.8 3.9 %collective-permute-done.4.refs_6_ = bf16[512,128]{1,0:T(8,128)(2,1)S(1)} collective-permute-done((bf16[512,128]{1,0:T(8,128)(2,1)S(1)}, bf16[512,128]{1,0:T(8,128)(2,1)S(1)}, u32[]{:S(2)}, u32[]{:S(2)}) %collective-permute-start.4) | collective-permute-done | bytes 131104 | tf_op jit(solution)/shard_map/ppermute | solution.py:217
  41.8 0.0 collective-permute-done.6.refs_8_
  41.8 5.7 %shard_map.84 = f32[1024,1024]{1,0:T(8,128)} custom-call(s32[1]{0:T(128)} %copy.14.live_ref, s32[2048]{0:T(1024)S(1)} %fusion.10.index_ref, bf16[512,512]{1,0:T(8,128)(2,1)S(1)} %copy-done.3, bf16[512,512]{1,0:T(8,128)(2,1)S(1)} %copy-done.2, bf16[512,128]{1,0:T(8,128)(2,1)S(1)} %get-tuple-element.13.refs_0_, ...), custom_call_target="tpu_custom_call" | custom-call | flops 6000000000 | bytes 6291456 | tf_op jit(solution)/shard_map/pallas_call | solution.py:238
  (16 shorter events, 0.0 us)
Async XLA Ops:
  0.0 0.9 %copy-start = (bf16[1024,64]{0,1:T(8,128)(2,1)S(1)}, bf16[1024,64]{0,1:T(8,128)(2,1)}, u32[]{:S(2)}) copy-start(bf16[1024,64]{0,1:T(8,128)(2,1)} %param.8) | copy-start | bytes 393220
  0.9 24.4 %copy-start.1 = (bf16[1024,1024]{1,0:T(8,128)(2,1)S(1)}, bf16[1024,1024]{1,0:T(8,128)(2,1)}, u32[]{:S(2)}) copy-start(bf16[1024,1024]{1,0:T(8,128)(2,1)} %constant.99.clone.forward_ref) | copy-start | bytes 6291460
  0.9 24.4 %copy-start.4 = (bf16[512,512]{1,0:T(8,128)(2,1)S(1)}, bf16[512,512]{1,0:T(8,128)(2,1)}, u32[]{:S(2)}) copy-start(bf16[512,512]{1,0:T(8,128)(2,1)} %constant.100.clone.band_ref) | copy-start | bytes 1572868
  0.9 24.4 %copy-start.5 = (f32[1,512]{1,0:T(1,128)S(1)}, f32[1,512]{1,0:T(1,128)}, u32[]{:S(2)}) copy-start(f32[1,512]{1,0:T(1,128)} %constant.101.clone.share_ref) | copy-start | bytes 6148
  1.1 36.6 %copy-start.6 = (s32[8,128,2]{1,2,0:T(2,128)S(1)}, s32[8,128,2]{1,2,0:T(2,128)}, u32[]{:S(2)}) copy-start(s32[8,128,2]{1,2,0:T(2,128)} %param.9) | copy-start | bytes 24580
  1.1 40.7 %copy-start.2 = (bf16[512,512]{1,0:T(8,128)(2,1)S(1)}, bf16[512,512]{1,0:T(8,128)(2,1)}, u32[]{:S(2)}) copy-start(bf16[512,512]{1,0:T(8,128)(2,1)} %constant.103.clone.odd_ref) | copy-start | bytes 1572868
  1.1 40.7 %copy-start.3 = (bf16[512,512]{1,0:T(8,128)(2,1)S(1)}, bf16[512,512]{1,0:T(8,128)(2,1)}, u32[]{:S(2)}) copy-start(bf16[512,512]{1,0:T(8,128)(2,1)} %constant.102.clone.even_ref) | copy-start | bytes 1572868
  26.4 6.4 %collective-permute-start.1 = (bf16[512,128]{1,0:T(8,128)(2,1)S(1)}, bf16[512,128]{1,0:T(8,128)(2,1)S(1)}, u32[]{:S(2)}, u32[]{:S(2)}) collective-permute-start(bf16[512,128]{1,0:T(8,128)(2,1)S(1)} %get-tuple-element.13.refs_0_), channel_id=1, source_target_pairs={{3,0},{0,1},{1,2},{2,3},{7,4},{4,5},{5,6},{6,7},{11,8},{8,9},{9,10... | collective-permute-start | bytes 393224 | tf_op jit(solution)/shard_map/ppermute | solution.py:217
  26.9 7.4 %collective-permute-start.3 = (bf16[512,128]{1,0:T(8,128)(2,1)S(1)}, bf16[512,128]{1,0:T(8,128)(2,1)S(1)}, u32[]{:S(2)}, u32[]{:S(2)}) collective-permute-start(bf16[512,128]{1,0:T(8,128)(2,1)S(1)} %get-tuple-element.11.refs_4_), channel_id=1, source_target_pairs={{1,0},{2,1},{3,2},{0,3},{5,4},{6,5},{7,6},{4,7},{9,8},{10,9},{11,1... | collective-permute-start | bytes 393224 | tf_op jit(solution)/shard_map/ppermute | solution.py:217
  28.5 7.1 %collective-permute-start.5 = (bf16[512,128]{1,0:T(8,128)(2,1)S(1)}, bf16[512,128]{1,0:T(8,128)(2,1)S(1)}, u32[]{:S(2)}, u32[]{:S(2)}) collective-permute-start(bf16[512,128]{1,0:T(8,128)(2,1)S(1)} %get-tuple-element.11.refs_4_), channel_id=1, source_target_pairs={{3,0},{0,1},{1,2},{2,3},{7,4},{4,5},{5,6},{6,7},{11,8},{8,9},{9,10... | collective-permute-start | bytes 393224 | tf_op jit(solution)/shard_map/ppermute | solution.py:217
  30.2 6.3 %collective-permute-start = (bf16[512,128]{1,0:T(8,128)(2,1)S(1)}, bf16[512,128]{1,0:T(8,128)(2,1)S(1)}, u32[]{:S(2)}, u32[]{:S(2)}) collective-permute-start(bf16[512,128]{1,0:T(8,128)(2,1)S(1)} %get-tuple-element.13.refs_0_), channel_id=1, source_target_pairs={{1,0},{2,1},{3,2},{0,3},{5,4},{6,5},{7,6},{4,7},{9,8},{10,9},{11,1... | collective-permute-start | bytes 393224 | tf_op jit(solution)/shard_map/ppermute | solution.py:217
  32.8 5.0 %collective-permute-start.2 = (bf16[512,128]{1,0:T(8,128)(2,1)S(1)}, bf16[512,128]{1,0:T(8,128)(2,1)S(1)}, u32[]{:S(2)}, u32[]{:S(2)}) collective-permute-start(bf16[512,128]{1,0:T(8,128)(2,1)S(1)} %collective-permute-done.1.refs_3_), channel_id=1, source_target_pairs={{3,0},{0,1},{1,2},{2,3},{7,4},{4,5},{5,6},{6,7},{11,8},{8,9},{9,10... | collective-permute-start | bytes 393224 | tf_op jit(solution)/shard_map/ppermute | solution.py:217
  34.3 7.5 %collective-permute-start.6 = (bf16[512,128]{1,0:T(8,128)(2,1)S(1)}, bf16[512,128]{1,0:T(8,128)(2,1)S(1)}, u32[]{:S(2)}, u32[]{:S(2)}) collective-permute-start(bf16[512,128]{1,0:T(8,128)(2,1)S(1)} %get-tuple-element.13.refs_0_), channel_id=1, source_target_pairs={{0,4},{4,0},{8,12},{12,8},{16,20},{20,16},{24,28},{28,24},{32,36},... | collective-permute-start | bytes 393224 | tf_op jit(solution)/shard_map/ppermute | solution.py:220
  34.4 7.4 %collective-permute-start.9 = (bf16[512,128]{1,0:T(8,128)(2,1)S(1)}, bf16[512,128]{1,0:T(8,128)(2,1)S(1)}, u32[]{:S(2)}, u32[]{:S(2)}) collective-permute-start(bf16[512,128]{1,0:T(8,128)(2,1)S(1)} %collective-permute-done.1.refs_3_), channel_id=1, source_target_pairs={{0,4},{4,0},{8,12},{12,8},{16,20},{20,16},{24,28},{28,24},{32,36},... | collective-permute-start | bytes 393224 | tf_op jit(solution)/shard_map/ppermute | solution.py:220
  35.6 6.2 %collective-permute-start.4 = (bf16[512,128]{1,0:T(8,128)(2,1)S(1)}, bf16[512,128]{1,0:T(8,128)(2,1)S(1)}, u32[]{:S(2)}, u32[]{:S(2)}) collective-permute-start(bf16[512,128]{1,0:T(8,128)(2,1)S(1)} %collective-permute-done.3.refs_5_), channel_id=1, source_target_pairs={{1,0},{2,1},{3,2},{0,3},{5,4},{6,5},{7,6},{4,7},{9,8},{10,9},{11,1... | collective-permute-start | bytes 393224 | tf_op jit(solution)/shard_map/ppermute | solution.py:217
  36.4 5.4 %collective-permute-start.7 = (bf16[512,128]{1,0:T(8,128)(2,1)S(1)}, bf16[512,128]{1,0:T(8,128)(2,1)S(1)}, u32[]{:S(2)}, u32[]{:S(2)}) collective-permute-start(bf16[512,128]{1,0:T(8,128)(2,1)S(1)} %collective-permute-done.refs_1_), channel_id=1, source_target_pairs={{0,4},{4,0},{8,12},{12,8},{16,20},{20,16},{24,28},{28,24},{32,36},... | collective-permute-start | bytes 393224 | tf_op jit(solution)/shard_map/ppermute | solution.py:220
  37.8 4.0 %collective-permute-start.8 = (bf16[512,128]{1,0:T(8,128)(2,1)S(1)}, bf16[512,128]{1,0:T(8,128)(2,1)S(1)}, u32[]{:S(2)}, u32[]{:S(2)}) collective-permute-start(bf16[512,128]{1,0:T(8,128)(2,1)S(1)} %collective-permute-done.2.refs_2_), channel_id=1, source_target_pairs={{0,4},{4,0},{8,12},{12,8},{16,20},{20,16},{24,28},{28,24},{32,36},... | collective-permute-start | bytes 393224 | tf_op jit(solution)/shard_map/ppermute | solution.py:220
